TPU v7x, 128 devices: a whole 4x4x4 slice. The times are simulated.
128 devices in a mesh: seq: 16 (over y, z_hi, core), head: 8 (over z_lo, x).
Axes of the slice: x: 4, y: 4, z: 4 (z_hi: 2, z_lo: 2; z = z_hi * 2 + z_lo), core: 2. Of those that a mesh axis runs over, the one named last changes fastest.
Arguments:
- query: bfloat16 [8192, 5120], P('seq', 'head'), may hold values from -6 to 6
- key_rows: bfloat16 [8192, 5120], P('seq', 'head'), may hold values from -6 to 6
- value_rows: bfloat16 [8192, 5120], P('seq', 'head'), may hold values from -6 to 6
- frame_seq: int32 [8192], replicated, may hold values from 0 to 3, never falling along the last dimension, each value on 1 to 3072 neighbouring positions
- order: int32 [32], replicated, may hold values from 0 to 31, each once
- w_out: bfloat16 [5120, 5120], P('head'), may hold values from -0.078125 to 0.078125
Outputs:
- mixed: bfloat16 [8192, 5120], P('seq', 'head')
Inputs may be any that keep to these rules, and one draw needn't show every extreme that they name: `frame_seq`: frames never fall along the sequence; each of the 4 frames holds 1 to 3072 tokens, and one holds exactly 3072. `order`: a permutation: every block number appears once.
All inputs are finite; a program needn't handle non-finite values.
Results may differ from a plain program's by a relative error of at most 0.019.
Values may be sent and summed in bfloat16 or wider, within the bound.
No kernel may reach another device: no remote copies, remote signals or barrier semaphores. Data moves between devices by JAX's collectives and lax.ppermute only.
A program may use at most 256 MiB of HBM per device.

v0:
```python
import functools
import math

import jax
import jax.numpy as jnp
from jax import lax
from jax.experimental import pallas as pl
from jax.experimental.pallas import tpu as pltpu
from jax.sharding import Mesh
from jax.sharding import PartitionSpec as P

HEAD_DIM = 128
HEADS = 5
WIDTH = HEADS * HEAD_DIM
BLOCK = 256
FRAMES = 4
BIG = 1e30
SCALE = HEAD_DIM ** (-0.5) * math.log2(math.e)
MIB = 1024 * 1024
SLOT = {(0, 0): 0, (0, 1): 2, (1, 0): 4, (3, 0): 6, (1, 1): 8, (3, 1): 10, (2, 0): 12, (2, 1): 14}
SMEM = pl.BlockSpec(memory_space=pltpu.SMEM)
VMEM = pl.BlockSpec(memory_space=pltpu.VMEM)
SMALL = pl.CostEstimate(flops=1024, bytes_accessed=1024, transcendentals=0)


def send(value, axis, step):
    size = {"y": 4, "x": 4}.get(axis, 2)
    return lax.ppermute(value, axis, [(i, (i + step) % size) for i in range(size)])


def after(value, *done):
    return lax.optimization_barrier((value, *done))[0]


def three_pieces(value):
    high = value.astype(jnp.bfloat16).astype(jnp.float32)
    rest = value - high
    middle = rest.astype(jnp.bfloat16).astype(jnp.float32)
    low = rest - middle
    return (high + pltpu.roll(middle, 8, 1) + pltpu.roll(low, 16, 1)).astype(jnp.bfloat16)


def tables_kernel(order_ref, frames_ref, k_mask_ref, q_frame_ref):
    y_at, zh_at, core_at = (lax.axis_index(a) for a in ("y", "zh", "core"))
    tokens = order_ref.shape[0] * BLOCK
    ends = []
    for f in range(FRAMES - 1):
        below = jnp.where(frames_ref[...] <= f, 1.0, 0.0)
        ends.append(jnp.sum(below).astype(jnp.int32))
    lane = lax.broadcasted_iota(jnp.int32, (BLOCK, HEAD_DIM), 1)
    offset = lax.broadcasted_iota(jnp.int32, (BLOCK, HEAD_DIM), 0)
    lane_end = jnp.where(
        lane == 0, ends[0], jnp.where(lane == 1, ends[1], jnp.where(lane == 2, ends[2], tokens))
    )
    lane_start = jnp.where(
        lane == 0, 0, jnp.where(lane == 1, ends[0], jnp.where(lane == 2, ends[1], ends[2]))
    )
    for (dy, dc), slot in SLOT.items():
        row = lax.rem(y_at + dy, 4)
        core = 1 - core_at if dc else core_at
        for half in range(2):
            token = order_ref[row * 8 + zh_at * 4 + core * 2 + half] * BLOCK + offset
            hidden = (token >= lane_end) & (lane < FRAMES)
            k_mask_ref[pl.ds((slot + half) * BLOCK, BLOCK), :] = jnp.where(
                hidden, -BIG, 0.0
            ).astype(jnp.bfloat16)
    for n in range(4):
        z = 1 - zh_at if n < 2 else zh_at
        token = order_ref[y_at * 8 + z * 4 + core_at * 2 + n % 2] * BLOCK + offset
        own = (token >= lane_start) & (token < lane_end) & (lane < FRAMES)
        q_frame_ref[pl.ds(n * BLOCK, BLOCK), :] = jnp.where(own, 1.0, 0.0).astype(jnp.bfloat16)


def tables(order, frames):
    return pl.pallas_call(
        tables_kernel,
        out_shape=(
            jax.ShapeDtypeStruct((4096, HEAD_DIM), jnp.bfloat16),
            jax.ShapeDtypeStruct((1024, HEAD_DIM), jnp.bfloat16),
        ),
        in_specs=[SMEM, VMEM],
        out_specs=(VMEM, VMEM),
        compiler_params=pltpu.CompilerParams(vmem_limit_bytes=8 * MIB),
        cost_estimate=SMALL,
    )(order, frames)


def attention_kernel(first, count_q, slots, state_at, last, k_mask, q_frame, *refs):
    q_parts, kv_parts = refs[:2], refs[2 : 2 + len(slots)]
    rest = refs[2 + len(slots) :]
    queries = count_q * BLOCK
    at = first * BLOCK
    rows_at = pl.ds(at, queries)
    if state_at is not None:
        o_in, log_in = rest[:2]
        rest = rest[2:]
        state_rows = pl.ds(at - state_at * BLOCK, queries)
    out = rest[0]
    hidden = jnp.concatenate(
        [k_mask[pl.ds(n * BLOCK, ref.shape[0]), :] for n, ref in zip(slots, kv_parts)], axis=0
    )
    keys = hidden.shape[0]
    own_frame = q_frame[rows_at, :]
    lane = lax.broadcasted_iota(jnp.int32, (queries, HEAD_DIM), 1)
    ones = jnp.ones((keys, HEAD_DIM), jnp.bfloat16)

    def columns(h, offset=0):
        return pl.ds(offset + h * HEAD_DIM, HEAD_DIM)

    def queries_of(h):
        taken = []
        for part, ref in enumerate(q_parts):
            low, high = max(at - part * 512, 0), min(at + queries - part * 512, 512)
            if low < high:
                taken.append(ref[pl.ds(low, high - low), columns(h)])
        return taken[0] if len(taken) == 1 else jnp.concatenate(taken, axis=0)

    def keys_of(h, offset):
        return jnp.concatenate([ref[:, columns(h, offset)] for ref in kv_parts], axis=0)

    def score(h):
        return lax.dot_general(
            jnp.concatenate([queries_of(h), own_frame], axis=1),
            jnp.concatenate([keys_of(h, 0), hidden], axis=1),
            (((1,), (1,)), ((), ())),
            preferred_element_type=jnp.float32,
        )

    def finish(h, acc, top, logs):
        value, total = acc[:, :HEAD_DIM], acc[:, HEAD_DIM:]
        top = jnp.broadcast_to(top * SCALE, (queries, HEAD_DIM))
        if state_at is not None:
            log = jnp.broadcast_to(log_in[state_rows, pl.ds(h, 1)], (queries, HEAD_DIM))
            both = jnp.maximum(log, top)
            new, old = jnp.exp2(top - both), jnp.exp2(log - both)
            value = value * new + o_in[state_rows, columns(h)] * old
            total = total * new + old
            top = both
        out[:, columns(h)] = (value / total).astype(out.dtype)
        return jnp.where(lane == h, top + jnp.log2(total), logs)

    logs = jnp.zeros((queries, HEAD_DIM), jnp.float32)
    scores, held = score(0), None
    for h in range(HEADS):
        ahead = score(h + 1) if h + 1 < HEADS else None
        top = jnp.max(scores, axis=1, keepdims=True)
        expo = jnp.exp2((scores - top) * SCALE).astype(jnp.bfloat16)
        values = jnp.concatenate([keys_of(h, WIDTH), ones], axis=1)
        acc = jnp.dot(expo, values, preferred_element_type=jnp.float32)
        if held is not None:
            logs = finish(h - 1, *held, logs)
        held, scores = (acc, top), ahead
    logs = finish(HEADS - 1, *held, logs)
    if last:
        out[:, pl.ds(WIDTH, HEAD_DIM)] = three_pieces(logs)
    else:
        rest[1][...] = logs


def attention(blocks, tabled, q_parts, kv_parts, state=(), state_at=0, last=False):
    first, count_q = blocks
    rows = count_q * BLOCK
    if last:
        out_shape = (jax.ShapeDtypeStruct((rows, WIDTH + HEAD_DIM), jnp.bfloat16),)
    else:
        out_shape = (
            jax.ShapeDtypeStruct((rows, WIDTH), jnp.float32),
            jax.ShapeDtypeStruct((rows, HEAD_DIM), jnp.float32),
        )
    slots = tuple(slot for slot, _ in kv_parts)
    return pl.pallas_call(
        functools.partial(
            attention_kernel, first, count_q, slots, state_at if state else None, last
        ),
        out_shape=out_shape,
        in_specs=[VMEM] * (4 + len(kv_parts) + len(state)),
        out_specs=(VMEM,) * len(out_shape),
        compiler_params=pltpu.CompilerParams(vmem_limit_bytes=30 * MIB),
        cost_estimate=SMALL,
    )(*tabled, *q_parts, *(part for _, part in kv_parts), *state)


def merge_kernel(mine, theirs, out):
    logs = []
    for ref in (mine, theirs):
        pieces = ref[:, pl.ds(WIDTH, HEAD_DIM)].astype(jnp.float32)
        logs.append(
            pieces + pltpu.roll(pieces, HEAD_DIM - 8, 1) + pltpu.roll(pieces, HEAD_DIM - 16, 1)
        )
    top = jnp.maximum(logs[0], logs[1])
    first, second = jnp.exp2(logs[0] - top), jnp.exp2(logs[1] - top)
    total = first + second
    first, second = first / total, second / total
    for h in range(HEADS):
        cols = pl.ds(h * HEAD_DIM, HEAD_DIM)
        out[:, cols] = (
            mine[:, cols].astype(jnp.float32) * first[:, h : h + 1]
            + theirs[:, cols].astype(jnp.float32) * second[:, h : h + 1]
        ).astype(jnp.bfloat16)


def merge(mine, theirs, block):
    full = WIDTH + HEAD_DIM
    return pl.pallas_call(
        merge_kernel,
        out_shape=jax.ShapeDtypeStruct((BLOCK, WIDTH), jnp.bfloat16),
        grid=(1,),
        in_specs=[
            pl.BlockSpec((BLOCK, full), lambda i: (block, 0)),
            pl.BlockSpec((BLOCK, full), lambda i: (0, 0)),
        ],
        out_specs=pl.BlockSpec((BLOCK, WIDTH), lambda i: (0, 0)),
        compiler_params=pltpu.CompilerParams(vmem_limit_bytes=8 * MIB),
        cost_estimate=SMALL,
    )(mine, theirs)


def join_kernel(k_ref, v_ref, out_ref, sem):
    copies = [
        pltpu.make_async_copy(ref, out_ref.at[:, pl.ds(n * WIDTH, WIDTH)], sem.at[n])
        for n, ref in enumerate((k_ref, v_ref))
    ]
    for copy in copies:
        copy.start()
    for copy in copies:
        copy.wait()


def join(keys, values):
    return pl.pallas_call(
        join_kernel,
        out_shape=jax.ShapeDtypeStruct((512, 2 * WIDTH), jnp.bfloat16),
        in_specs=[pl.BlockSpec(memory_space=pl.ANY)] * 2,
        out_specs=VMEM,
        scratch_shapes=[pltpu.SemaphoreType.DMA((2,))],
        compiler_params=pltpu.CompilerParams(vmem_limit_bytes=8 * MIB),
        cost_estimate=SMALL,
    )(keys, values)


def project_kernel(give, *refs):
    mine, other, parts, out_ref = refs[:4], refs[4:8], refs[8:13], refs[13]
    core_at, zl_at = lax.axis_index("core"), lax.axis_index("zl")

    def run(weights):
        rows = [
            parts[0][...],
            parts[1][...],
            jnp.concatenate([parts[2][...], parts[3][...]], axis=0),
            parts[4][...],
        ]
        total = None
        for row, w in zip(rows, weights):
            term = jnp.dot(row, w[...], preferred_element_type=jnp.float32)
            total = term if total is None else total + term
        out_ref[...] = total.astype(out_ref.dtype)

    same = core_at == zl_at

    @pl.when(same != give)
    def _():
        run(mine)

    @pl.when(same == give)
    def _():
        run(other)


def project(give, w_mine, w_other, parts, dtype):
    return pl.pallas_call(
        functools.partial(project_kernel, give),
        out_shape=jax.ShapeDtypeStruct((BLOCK, 640), dtype),
        in_specs=[VMEM] * 13,
        out_specs=VMEM,
        compiler_params=pltpu.CompilerParams(vmem_limit_bytes=12 * MIB),
        cost_estimate=SMALL,
    )(*w_mine, *w_other, *parts)


def together(*groups):
    flat, tree = jax.tree.flatten(groups)
    return jax.tree.unflatten(tree, lax.optimization_barrier(tuple(flat)))


def on_device(query, key_rows, value_rows, frame_seq, order, w_out):
    core_at, x_at = lax.axis_index("core"), lax.axis_index("x")

    def columns(zl, distance):
        return lax.dynamic_slice_in_dim(w_out, (zl * 4 + (x_at + distance) % 4) * 640, 640, 1)

    kv = join(key_rows, value_rows)
    kv_next = send(kv, "y", -1)
    kv_back = send(kv, "y", 1)
    q_z = send(query, "zh", 1)
    kv_core = send(kv, "core", 1)
    w_next = send(after(columns(core_at, 3), kv_core), "x", -1)
    w_back = send(after(columns(core_at, 1), kv_core), "x", 1)
    attend = functools.partial(
        attention, tabled=tables(order, frame_seq.reshape(64, 128)), q_parts=(q_z, query)
    )
    state = attend((0, 4), kv_parts=((0, kv), (2, kv_core)))
    kv_next, kv_back, w_next, w_back, state = together(kv_next, kv_back, w_next, w_back, state)

    far_low = send(kv_next[:BLOCK], "y", -1)
    far_high = send(kv_back[BLOCK:], "y", 1)
    next_core = send(kv_next, "core", 1)
    back_core = send(kv_back, "core", 1)
    w_far = send(after(columns(core_at, 2), w_next), "x", 2)
    state = attend((0, 4), kv_parts=((4, kv_next), (6, kv_back)), state=state)
    cores = ((8, next_core), (10, back_core))
    state_z = attend((0, 2), kv_parts=cores, state=state)
    far_low, far_high, state_z = together(far_low, far_high, state_z)

    low_core, high_core = send(far_low, "core", 1), send(far_high, "core", 1)
    w_next_core, w_back_core = send(w_next, "core", 1), send(w_back, "core", 1)
    far = ((12, far_low), (13, far_high))
    state_z = attend((0, 2), kv_parts=far, state=state_z)
    low_core, high_core, w_far, state_z = together(low_core, high_core, w_far, state_z)
    far_core = ((14, low_core), (15, high_core))
    w_far_core = send(w_far, "core", 1)
    got = []
    for block in range(2):
        (give,) = attend((block, 1), kv_parts=far_core, state=state_z, last=True)
        got.append(send(give, "zh", 1))
        state, give = together(state, give)
    state = attend((2, 2), kv_parts=cores, state=state)
    (keep,) = attend((2, 2), kv_parts=far + far_core, state=state, state_at=2, last=True)
    keep, w_next_core, w_back_core, w_far_core = together(
        keep, w_next_core, w_back_core, w_far_core
    )
    w_mine = (columns(core_at, 0), w_next, w_far, w_back)
    w_other = (columns(1 - core_at, 0), w_next_core, w_far_core, w_back_core)

    out = []
    for block, their in enumerate(got):
        done = merge(keep, their, block)
        one, three = send(done, "x", -1), send(done, "x", 1)
        low, high = send(one[:128], "x", -1), send(three[128:], "x", 1)
        out.append([done, one, low, high, three])

    came = [
        send(project(True, w_mine, w_other, parts, jnp.bfloat16), "zl", 1) for parts in out
    ]
    kept = [project(False, w_mine, w_other, parts, jnp.float32) for parts in out]
    return jnp.concatenate(
        [(a + b.astype(jnp.float32)).astype(jnp.bfloat16) for a, b in zip(kept, came)], axis=0
    )


def solution(mesh):
    fine = Mesh(mesh.devices.reshape(4, 2, 2, 2, 4), ("y", "zh", "core", "zl", "x"))
    rows, columns = ("y", "zh", "core"), ("zl", "x")
    return jax.shard_map(
        on_device,
        mesh=fine,
        in_specs=(P(rows, columns),) * 3 + (P(), P(), P(columns, None)),
        out_specs=P(rows, columns),
        check_vma=False,
    )
```

profile of v0, /device:TPU:0, one launch (start us, length us, event | category | flops | bytes accessed | tf_op | source)
XLA Modules:
  0.0 135.8 jit_solution(11114973152941730661)
XLA Ops:
  2.4 3.2 %collective-permute-start = (bf16[512,1280]{1,0:T(8,128)(2,1)S(1)}, bf16[512,1280]{1,0:T(8,128)(2,1)S(1)}, u32[]{:S(2)}, u32[]{:S(2)}) collective-permute-start(bf16[512,1280]{1,0:T(8,128)(2,1)S(1)} %shard_map.64.refs_2_), channel_id=1, source_target_pairs={{0,96},{32,0},{64,32},{96,64},{1,97},{33,1},{65,33},{97,65},{2,98}... | collective-permute-start | bytes 3932168 | tf_op jit(solution)/shard_map/ppermute | solution.py:28
  5.6 2.6 %constant_dynamic-slice_fusion = (bf16[640,640]{1,0:T(8,128)(2,1)S(1)}, bf16[640,640]{1,0:T(8,128)(2,1)S(1)}, bf16[640,640]{1,0:T(8,128)(2,1)S(1)}, bf16[640,640]{1,0:T(8,128)(2,1)S(1)}, bf16[640,640]{1,0:T(8,128)(2,1)S(1)}) fusion(bf16[640,5120]{1,0:T(8,128)(2,1)} %param.11, s32[]{:T(128)S(6)} %select_n.44, s32[]{:T(128)S(6)} %select_n.41, s32[]{:T(128)S(6)} %select_n.39, ...), kind=kLoop, calls=%fused_computation.3 | loop fusion | bytes 8192020 | tf_op jit(solution)/shard_map/dynamic_slice | solution.py:289
  8.2 2.8 %collective-permute-start.3 = (bf16[640,640]{1,0:T(8,128)(2,1)S(1)}, bf16[640,640]{1,0:T(8,128)(2,1)S(1)}, u32[]{:S(2)}, u32[]{:S(2)}) collective-permute-start(bf16[640,640]{1,0:T(8,128)(2,1)S(1)} %get-tuple-element.43), channel_id=1, source_target_pairs={{0,3},{1,0},{2,1},{3,2},{4,7},{5,4},{6,5},{7,6},{8,11},{9,8},{10,9... | collective-permute-start | bytes 2457608 | tf_op jit(solution)/shard_map/ppermute | solution.py:28
  11.0 3.9 %collective-permute-start.5 = (bf16[512,640]{1,0:T(8,128)(2,1)S(1)}, bf16[512,640]{1,0:T(8,128)(2,1)S(1)}, u32[]{:S(2)}, u32[]{:S(2)}) collective-permute-start(bf16[512,640]{1,0:T(8,128)(2,1)S(1)} %copy-done), channel_id=1, source_target_pairs={{0,16},{16,0},{1,17},{17,1},{2,18},{18,2},{3,19},{19,3},{4,20},{20... | collective-permute-start | bytes 1966088 | tf_op jit(solution)/shard_map/ppermute | solution.py:28
  16.0 13.7 %collective-permute-done.5.refs_0_ = bf16[512,640]{1,0:T(8,128)(2,1)S(1)} collective-permute-done((bf16[512,640]{1,0:T(8,128)(2,1)S(1)}, bf16[512,640]{1,0:T(8,128)(2,1)S(1)}, u32[]{:S(2)}, u32[]{:S(2)}) %collective-permute-start.5) | collective-permute-done | bytes 655392 | tf_op jit(solution)/shard_map/ppermute | solution.py:28
  29.7 8.0 %shard_map.66 = (f32[1024,640]{1,0:T(8,128)S(1)}, f32[1024,128]{1,0:T(8,128)S(1)}) custom-call(bf16[4096,128]{1,0:T(8,128)(2,1)S(1)} %get-tuple-element.45.k_mask, bf16[1024,128]{1,0:T(8,128)(2,1)S(1)} %get-tuple-element.46.q_frame, bf16[512,640]{1,0:T(8,128)(2,1)S(1)} %collective-permute-done.5.refs_0_, bf16[512,640]{1,0:T(8,128)(2,1)S(1)} %copy-done, ...), custom_call_target="tpu_custom_call" | custom-call | flops 1024 | bytes 1024 | tf_op jit(solution)/shard_map/pallas_call | solution.py:171
  39.5 3.0 %collective-permute-start.6 = (bf16[256,1280]{1,0:T(8,128)(2,1)S(1)}, bf16[256,1280]{1,0:T(8,128)(2,1)S(1)}, u32[]{:S(2)}, u32[]{:S(2)}) collective-permute-start(bf16[256,1280]{1,0:T(8,128)(2,1)S(1)} %slice.18), channel_id=1, source_target_pairs={{0,96},{32,0},{64,32},{96,64},{1,97},{33,1},{65,33},{97,65},{2,98}... | collective-permute-start | bytes 1966088 | tf_op jit(solution)/shard_map/ppermute | solution.py:28
  42.5 14.1 %collective-permute-start.12 = (bf16[640,640]{1,0:T(8,128)(2,1)S(1)}, bf16[640,640]{1,0:T(8,128)(2,1)S(1)}, u32[]{:S(2)}, u32[]{:S(2)}) collective-permute-start(bf16[640,640]{1,0:T(8,128)(2,1)S(1)} %get-tuple-element.60), channel_id=1, source_target_pairs={{0,2},{1,3},{2,0},{3,1},{4,6},{5,7},{6,4},{7,5},{8,10},{9,11},{10,... | collective-permute-start | bytes 2457608 | tf_op jit(solution)/shard_map/ppermute | solution.py:28
  56.6 8.6 %shard_map.67 = (f32[1024,640]{1,0:T(8,128)S(1)}, f32[1024,128]{1,0:T(8,128)S(1)}) custom-call(bf16[4096,128]{1,0:T(8,128)(2,1)S(1)} %get-tuple-element.45.k_mask, bf16[1024,128]{1,0:T(8,128)(2,1)S(1)} %get-tuple-element.46.q_frame, bf16[512,640]{1,0:T(8,128)(2,1)S(1)} %collective-permute-done.5.refs_0_, bf16[512,640]{1,0:T(8,128)(2,1)S(1)} %copy-done, ...), custom_call_target="tpu_custom_call" | custom-call | flops 1024 | bytes 1024 | tf_op jit(solution)/shard_map/pallas_call | solution.py:171
  65.2 3.9 %shard_map.68 = (f32[512,640]{1,0:T(8,128)S(1)}, f32[512,128]{1,0:T(8,128)S(1)}) custom-call(bf16[4096,128]{1,0:T(8,128)(2,1)S(1)} %get-tuple-element.45.k_mask, bf16[1024,128]{1,0:T(8,128)(2,1)S(1)} %get-tuple-element.46.q_frame, bf16[512,640]{1,0:T(8,128)(2,1)S(1)} %collective-permute-done.5.refs_0_, bf16[512,640]{1,0:T(8,128)(2,1)S(1)} %copy-done, ...), custom_call_target="tpu_custom_call" | custom-call | flops 1024 | bytes 1024 | tf_op jit(solution)/shard_map/pallas_call | solution.py:171
  70.2 2.1 %shard_map.69 = (f32[512,640]{1,0:T(8,128)S(1)}, f32[512,128]{1,0:T(8,128)S(1)}) custom-call(bf16[4096,128]{1,0:T(8,128)(2,1)S(1)} %get-tuple-element.45.k_mask, bf16[1024,128]{1,0:T(8,128)(2,1)S(1)} %get-tuple-element.46.q_frame, bf16[512,640]{1,0:T(8,128)(2,1)S(1)} %collective-permute-done.5.refs_0_, bf16[512,640]{1,0:T(8,128)(2,1)S(1)} %copy-done, ...), custom_call_target="tpu_custom_call" | custom-call | flops 1024 | bytes 1024 | tf_op jit(solution)/shard_map/pallas_call | solution.py:171
  72.3 3.7 %collective-permute-done.12.refs_2_ = bf16[640,640]{1,0:T(8,128)(2,1)S(1)} collective-permute-done((bf16[640,640]{1,0:T(8,128)(2,1)S(1)}, bf16[640,640]{1,0:T(8,128)(2,1)S(1)}, u32[]{:S(2)}, u32[]{:S(2)}) %collective-permute-start.12) | collective-permute-done | bytes 819232 | tf_op jit(solution)/shard_map/ppermute | solution.py:28
  76.0 1.4 %shard_map.70 = bf16[256,768]{1,0:T(8,128)(2,1)S(1)} custom-call(bf16[4096,128]{1,0:T(8,128)(2,1)S(1)} %get-tuple-element.45.k_mask, bf16[1024,128]{1,0:T(8,128)(2,1)S(1)} %get-tuple-element.46.q_frame, bf16[512,640]{1,0:T(8,128)(2,1)S(1)} %collective-permute-done.5.refs_0_, bf16[512,640]{1,0:T(8,128)(2,1)S(1)} %copy-done, ...), custom_call_target="tpu_custom_call" | custom-call | flops 1024 | bytes 1024 | tf_op jit(solution)/shard_map/pallas_call | solution.py:171
  77.4 3.3 %collective-permute-start.16 = (bf16[256,768]{1,0:T(8,128)(2,1)S(1)}, bf16[256,768]{1,0:T(8,128)(2,1)S(1)}, u32[]{:S(2)}, u32[]{:S(2)}) collective-permute-start(bf16[256,768]{1,0:T(8,128)(2,1)S(1)} %shard_map.70), channel_id=1, source_target_pairs={{0,16},{16,0},{1,17},{17,1},{2,18},{18,2},{3,19},{19,3},{4,20},{20... | collective-permute-start | bytes 1179656 | tf_op jit(solution)/shard_map/ppermute | solution.py:28
  80.7 1.4 %shard_map.71 = bf16[256,768]{1,0:T(8,128)(2,1)S(1)} custom-call(bf16[4096,128]{1,0:T(8,128)(2,1)S(1)} %get-tuple-element.45.k_mask, bf16[1024,128]{1,0:T(8,128)(2,1)S(1)} %get-tuple-element.46.q_frame, bf16[512,640]{1,0:T(8,128)(2,1)S(1)} %collective-permute-done.5.refs_0_, bf16[512,640]{1,0:T(8,128)(2,1)S(1)} %copy-done, ...), custom_call_target="tpu_custom_call" | custom-call | flops 1024 | bytes 1024 | tf_op jit(solution)/shard_map/pallas_call | solution.py:171
  82.9 3.9 %shard_map.72 = (f32[512,640]{1,0:T(8,128)S(1)}, f32[512,128]{1,0:T(8,128)S(1)}) custom-call(bf16[4096,128]{1,0:T(8,128)(2,1)S(1)} %get-tuple-element.45.k_mask, bf16[1024,128]{1,0:T(8,128)(2,1)S(1)} %get-tuple-element.46.q_frame, bf16[512,640]{1,0:T(8,128)(2,1)S(1)} %collective-permute-done.5.refs_0_, bf16[512,640]{1,0:T(8,128)(2,1)S(1)} %copy-done, ...), custom_call_target="tpu_custom_call" | custom-call | flops 1024 | bytes 1024 | tf_op jit(solution)/shard_map/pallas_call | solution.py:171
  86.8 4.0 %shard_map.73.mine = bf16[512,768]{1,0:T(8,128)(2,1)S(1)} custom-call(bf16[4096,128]{1,0:T(8,128)(2,1)S(1)} %get-tuple-element.45.k_mask, bf16[1024,128]{1,0:T(8,128)(2,1)S(1)} %get-tuple-element.46.q_frame, bf16[512,640]{1,0:T(8,128)(2,1)S(1)} %collective-permute-done.5.refs_0_, bf16[512,640]{1,0:T(8,128)(2,1)S(1)} %copy-done, ...), custom_call_target="tpu_custom_call" | custom-call | flops 1024 | bytes 1024 | tf_op jit(solution)/shard_map/pallas_call | solution.py:171
  91.5 3.0 %collective-permute-start.17 = (bf16[256,640]{1,0:T(8,128)(2,1)S(1)}, bf16[256,640]{1,0:T(8,128)(2,1)S(1)}, u32[]{:S(2)}, u32[]{:S(2)}) collective-permute-start(bf16[256,640]{1,0:T(8,128)(2,1)S(1)} %shard_map.74.refs_8_), channel_id=1, source_target_pairs={{0,3},{1,0},{2,1},{3,2},{4,7},{5,4},{6,5},{7,6},{8,11},{9,8},{10,9... | collective-permute-start | bytes 983048 | tf_op jit(solution)/shard_map/ppermute | solution.py:28
  94.5 4.4 %collective-permute-done.22.theirs = bf16[256,768]{1,0:T(8,128)(2,1)S(1)} collective-permute-done((bf16[256,768]{1,0:T(8,128)(2,1)S(1)}, bf16[256,768]{1,0:T(8,128)(2,1)S(1)}, u32[]{:S(2)}, u32[]{:S(2)}) %collective-permute-start.22) | collective-permute-done | bytes 393248 | tf_op jit(solution)/shard_map/ppermute | solution.py:28
  99.5 3.0 %collective-permute-start.23 = (bf16[256,640]{1,0:T(8,128)(2,1)S(1)}, bf16[256,640]{1,0:T(8,128)(2,1)S(1)}, u32[]{:S(2)}, u32[]{:S(2)}) collective-permute-start(bf16[256,640]{1,0:T(8,128)(2,1)S(1)} %shard_map.77.refs_8_), channel_id=1, source_target_pairs={{0,3},{1,0},{2,1},{3,2},{4,7},{5,4},{6,5},{7,6},{8,11},{9,8},{10,9... | collective-permute-start | bytes 983048 | tf_op jit(solution)/shard_map/ppermute | solution.py:28
  102.6 3.3 %collective-permute-start.18 = (bf16[128,640]{1,0:T(8,128)(2,1)S(1)}, bf16[128,640]{1,0:T(8,128)(2,1)S(1)}, u32[]{:S(2)}, u32[]{:S(2)}) collective-permute-start(bf16[128,640]{1,0:T(8,128)(2,1)S(1)} %slice.24), channel_id=1, source_target_pairs={{0,3},{1,0},{2,1},{3,2},{4,7},{5,4},{6,5},{7,6},{8,11},{9,8},{10,9... | collective-permute-start | bytes 491528 | tf_op jit(solution)/shard_map/ppermute | solution.py:28
  106.0 6.9 %collective-permute-done.18.refs_10_ = bf16[128,640]{1,0:T(8,128)(2,1)S(1)} collective-permute-done((bf16[128,640]{1,0:T(8,128)(2,1)S(1)}, bf16[128,640]{1,0:T(8,128)(2,1)S(1)}, u32[]{:S(2)}, u32[]{:S(2)}) %collective-permute-start.18) | collective-permute-done | bytes 163872 | tf_op jit(solution)/shard_map/ppermute | solution.py:28
  112.9 3.4 %collective-permute-done.20.refs_11_ = bf16[128,640]{1,0:T(8,128)(2,1)S(1)} collective-permute-done((bf16[128,640]{1,0:T(8,128)(2,1)S(1)}, bf16[128,640]{1,0:T(8,128)(2,1)S(1)}, u32[]{:S(2)}, u32[]{:S(2)}) %collective-permute-start.20) | collective-permute-done | bytes 163872 | tf_op jit(solution)/shard_map/ppermute | solution.py:28
  116.3 1.5 %shard_map.76 = bf16[256,640]{1,0:T(8,128)(2,1)S(1)} custom-call(bf16[640,640]{1,0:T(8,128)(2,1)S(1)} %get-tuple-element.84.refs_0_, bf16[640,640]{1,0:T(8,128)(2,1)S(1)} %collective-permute-done.3.refs_1_, bf16[640,640]{1,0:T(8,128)(2,1)S(1)} %collective-permute-done.12.refs_2_, bf16[640,640]{1,0:T(8,128)(2,1)S(1)} %collective-permute-done.4.refs_3_, ...), custom_call_target="tpu_custom_call" | custom-call | flops 1024 | bytes 1024 | tf_op jit(solution)/shard_map/pallas_call | solution.py:270
  117.8 1.4 %collective-permute-start.21 = (bf16[256,640]{1,0:T(8,128)(2,1)S(1)}, bf16[256,640]{1,0:T(8,128)(2,1)S(1)}, u32[]{:S(2)}, u32[]{:S(2)}) collective-permute-start(bf16[256,640]{1,0:T(8,128)(2,1)S(1)} %shard_map.76), channel_id=1, source_target_pairs={{0,4},{4,0},{1,5},{5,1},{2,6},{6,2},{3,7},{7,3},{8,12},{12,8},{9,1... | collective-permute-start | bytes 983048 | tf_op jit(solution)/shard_map/ppermute | solution.py:28
  119.6 1.8 %collective-permute-start.26 = (bf16[128,640]{1,0:T(8,128)(2,1)S(1)}, bf16[128,640]{1,0:T(8,128)(2,1)S(1)}, u32[]{:S(2)}, u32[]{:S(2)}) collective-permute-start(bf16[128,640]{1,0:T(8,128)(2,1)S(1)} %slice.27), channel_id=1, source_target_pairs={{0,1},{1,2},{2,3},{3,0},{4,5},{5,6},{6,7},{7,4},{8,9},{9,10},{10,1... | collective-permute-start | bytes 491528 | tf_op jit(solution)/shard_map/ppermute | solution.py:28
  121.4 3.2 %collective-permute-done.24.refs_10_ = bf16[128,640]{1,0:T(8,128)(2,1)S(1)} collective-permute-done((bf16[128,640]{1,0:T(8,128)(2,1)S(1)}, bf16[128,640]{1,0:T(8,128)(2,1)S(1)}, u32[]{:S(2)}, u32[]{:S(2)}) %collective-permute-start.24) | collective-permute-done | bytes 163872 | tf_op jit(solution)/shard_map/ppermute | solution.py:28
  124.6 1.6 %collective-permute-done.26.refs_11_ = bf16[128,640]{1,0:T(8,128)(2,1)S(1)} collective-permute-done((bf16[128,640]{1,0:T(8,128)(2,1)S(1)}, bf16[128,640]{1,0:T(8,128)(2,1)S(1)}, u32[]{:S(2)}, u32[]{:S(2)}) %collective-permute-start.26) | collective-permute-done | bytes 163872 | tf_op jit(solution)/shard_map/ppermute | solution.py:28
  126.2 1.3 shard_map.79
  128.3 1.3 shard_map.75
  129.6 1.3 shard_map.78
  131.1 3.6 %collective-permute-done.27 = bf16[256,640]{1,0:T(8,128)(2,1)S(1)} collective-permute-done((bf16[256,640]{1,0:T(8,128)(2,1)S(1)}, bf16[256,640]{1,0:T(8,128)(2,1)S(1)}, u32[]{:S(2)}, u32[]{:S(2)}) %collective-permute-start.27) | collective-permute-done | bytes 327712 | tf_op jit(solution)/shard_map/ppermute | solution.py:28
  (60 shorter events, 10.7 us)
Async XLA Ops:
  0.0 1.1 copy-start.1
  2.3 5.9 %collective-permute-start.2 = (bf16[512,1280]{1,0:T(8,128)(2,1)S(1)}, bf16[512,1280]{1,0:T(8,128)(2,1)}, u32[]{:S(2)}, u32[]{:S(2)}) collective-permute-start(bf16[512,1280]{1,0:T(8,128)(2,1)S(1)} %shard_map.64.refs_2_), channel_id=1, source_target_pairs={{0,8},{8,0},{1,9},{9,1},{2,10},{10,2},{3,11},{11,3},{4,12},{12,4},... | collective-permute-start | bytes 3932168 | tf_op jit(solution)/shard_map/ppermute | solution.py:28
  2.4 35.3 %collective-permute-start = (bf16[512,1280]{1,0:T(8,128)(2,1)S(1)}, bf16[512,1280]{1,0:T(8,128)(2,1)S(1)}, u32[]{:S(2)}, u32[]{:S(2)}) collective-permute-start(bf16[512,1280]{1,0:T(8,128)(2,1)S(1)} %shard_map.64.refs_2_), channel_id=1, source_target_pairs={{0,96},{32,0},{64,32},{96,64},{1,97},{33,1},{65,33},{97,65},{2,98}... | collective-permute-start | bytes 3932168 | tf_op jit(solution)/shard_map/ppermute | solution.py:28
  5.6 32.2 %collective-permute-start.1 = (bf16[512,1280]{1,0:T(8,128)(2,1)S(1)}, bf16[512,1280]{1,0:T(8,128)(2,1)}, u32[]{:S(2)}, u32[]{:S(2)}) collective-permute-start(bf16[512,1280]{1,0:T(8,128)(2,1)S(1)} %shard_map.64.refs_2_), channel_id=1, source_target_pairs={{0,32},{32,64},{64,96},{96,0},{1,33},{33,65},{65,97},{97,1},{2,34}... | collective-permute-start | bytes 3932168 | tf_op jit(solution)/shard_map/ppermute | solution.py:28
  5.6 5.4 %copy-start = (bf16[512,640]{1,0:T(8,128)(2,1)S(1)}, bf16[512,640]{1,0:T(8,128)(2,1)}, u32[]{:S(2)}) copy-start(bf16[512,640]{1,0:T(8,128)(2,1)} %refs_1_.15) | copy-start | bytes 1966084
  5.6 9.3 %copy-start.3 = (s32[8192]{0:T(1024)S(1)}, s32[8192]{0:T(1024)}, u32[]{:S(2)}) copy-start(s32[8192]{0:T(1024)} %param.9) | copy-start | bytes 98308
  5.6 9.3 %copy-start.4 = (s32[32]{0:T(128)S(1)}, s32[32]{0:T(128)}, u32[]{:S(2)}) copy-start(s32[32]{0:T(128)} %order_ref.1) | copy-start | bytes 388
  8.2 29.6 %collective-permute-start.3 = (bf16[640,640]{1,0:T(8,128)(2,1)S(1)}, bf16[640,640]{1,0:T(8,128)(2,1)S(1)}, u32[]{:S(2)}, u32[]{:S(2)}) collective-permute-start(bf16[640,640]{1,0:T(8,128)(2,1)S(1)} %get-tuple-element.43), channel_id=1, source_target_pairs={{0,3},{1,0},{2,1},{3,2},{4,7},{5,4},{6,5},{7,6},{8,11},{9,8},{10,9... | collective-permute-start | bytes 2457608 | tf_op jit(solution)/shard_map/ppermute | solution.py:28
  11.0 26.7 %collective-permute-start.4 = (bf16[640,640]{1,0:T(8,128)(2,1)S(1)}, bf16[640,640]{1,0:T(8,128)(2,1)S(1)}, u32[]{:S(2)}, u32[]{:S(2)}) collective-permute-start(bf16[640,640]{1,0:T(8,128)(2,1)S(1)} %get-tuple-element.44), channel_id=1, source_target_pairs={{0,1},{1,2},{2,3},{3,0},{4,5},{5,6},{6,7},{7,4},{8,9},{9,10},{10,1... | collective-permute-start | bytes 2457608 | tf_op jit(solution)/shard_map/ppermute | solution.py:28
  11.0 18.7 %collective-permute-start.5 = (bf16[512,640]{1,0:T(8,128)(2,1)S(1)}, bf16[512,640]{1,0:T(8,128)(2,1)S(1)}, u32[]{:S(2)}, u32[]{:S(2)}) collective-permute-start(bf16[512,640]{1,0:T(8,128)(2,1)S(1)} %copy-done), channel_id=1, source_target_pairs={{0,16},{16,0},{1,17},{17,1},{2,18},{18,2},{3,19},{19,3},{4,20},{20... | collective-permute-start | bytes 1966088 | tf_op jit(solution)/shard_map/ppermute | solution.py:28
  37.7 27.4 %collective-permute-start.8 = (bf16[512,1280]{1,0:T(8,128)(2,1)S(1)}, bf16[512,1280]{1,0:T(8,128)(2,1)S(1)}, u32[]{:S(2)}, u32[]{:S(2)}) collective-permute-start(bf16[512,1280]{1,0:T(8,128)(2,1)S(1)} %collective-permute-done.refs_2_), channel_id=1, source_target_pairs={{0,8},{8,0},{1,9},{9,1},{2,10},{10,2},{3,11},{11,3},{4,12},{12,4},... | collective-permute-start | bytes 3932168 | tf_op jit(solution)/shard_map/ppermute | solution.py:28
  37.8 27.3 %collective-permute-start.9 = (bf16[512,1280]{1,0:T(8,128)(2,1)}, bf16[512,1280]{1,0:T(8,128)(2,1)S(1)}, u32[]{:S(2)}, u32[]{:S(2)}) collective-permute-start(bf16[512,1280]{1,0:T(8,128)(2,1)} %collective-permute-done.1.refs_3_), channel_id=1, source_target_pairs={{0,8},{8,0},{1,9},{9,1},{2,10},{10,2},{3,11},{11,3},{4,12},{12,4},... | collective-permute-start | bytes 3932168 | tf_op jit(solution)/shard_map/ppermute | solution.py:28
  39.5 29.5 %collective-permute-start.6 = (bf16[256,1280]{1,0:T(8,128)(2,1)S(1)}, bf16[256,1280]{1,0:T(8,128)(2,1)S(1)}, u32[]{:S(2)}, u32[]{:S(2)}) collective-permute-start(bf16[256,1280]{1,0:T(8,128)(2,1)S(1)} %slice.18), channel_id=1, source_target_pairs={{0,96},{32,0},{64,32},{96,64},{1,97},{33,1},{65,33},{97,65},{2,98}... | collective-permute-start | bytes 1966088 | tf_op jit(solution)/shard_map/ppermute | solution.py:28
  42.5 26.5 %collective-permute-start.7 = (bf16[256,1280]{1,0:T(8,128)(2,1)S(1)}, bf16[256,1280]{1,0:T(8,128)(2,1)S(1)}, u32[]{:S(2)}, u32[]{:S(2)}) collective-permute-start(bf16[256,1280]{1,0:T(8,128)(2,1)S(1)} %slice.19), channel_id=1, source_target_pairs={{0,32},{32,64},{64,96},{96,0},{1,33},{33,65},{65,97},{97,1},{2,34}... | collective-permute-start | bytes 1966088 | tf_op jit(solution)/shard_map/ppermute | solution.py:28
  42.5 33.5 %collective-permute-start.12 = (bf16[640,640]{1,0:T(8,128)(2,1)S(1)}, bf16[640,640]{1,0:T(8,128)(2,1)S(1)}, u32[]{:S(2)}, u32[]{:S(2)}) collective-permute-start(bf16[640,640]{1,0:T(8,128)(2,1)S(1)} %get-tuple-element.60), channel_id=1, source_target_pairs={{0,2},{1,3},{2,0},{3,1},{4,6},{5,7},{6,4},{7,5},{8,10},{9,11},{10,... | collective-permute-start | bytes 2457608 | tf_op jit(solution)/shard_map/ppermute | solution.py:28
  69.1 6.9 %collective-permute-start.10 = (bf16[256,1280]{1,0:T(8,128)(2,1)S(1)}, bf16[256,1280]{1,0:T(8,128)(2,1)S(1)}, u32[]{:S(2)}, u32[]{:S(2)}) collective-permute-start(bf16[256,1280]{1,0:T(8,128)(2,1)S(1)} %collective-permute-done.6.refs_2_), channel_id=1, source_target_pairs={{0,8},{8,0},{1,9},{9,1},{2,10},{10,2},{3,11},{11,3},{4,12},{12,4},... | collective-permute-start | bytes 1966088 | tf_op jit(solution)/shard_map/ppermute | solution.py:28
  69.2 6.9 %collective-permute-start.11 = (bf16[256,1280]{1,0:T(8,128)(2,1)S(1)}, bf16[256,1280]{1,0:T(8,128)(2,1)S(1)}, u32[]{:S(2)}, u32[]{:S(2)}) collective-permute-start(bf16[256,1280]{1,0:T(8,128)(2,1)S(1)} %collective-permute-done.7.refs_3_), channel_id=1, source_target_pairs={{0,8},{8,0},{1,9},{9,1},{2,10},{10,2},{3,11},{11,3},{4,12},{12,4},... | collective-permute-start | bytes 1966088 | tf_op jit(solution)/shard_map/ppermute | solution.py:28
  69.7 21.1 %collective-permute-start.13 = (bf16[640,640]{1,0:T(8,128)(2,1)S(1)}, bf16[640,640]{1,0:T(8,128)(2,1)S(1)}, u32[]{:S(2)}, u32[]{:S(2)}) collective-permute-start(bf16[640,640]{1,0:T(8,128)(2,1)S(1)} %collective-permute-done.3.refs_1_), channel_id=1, source_target_pairs={{0,8},{8,0},{1,9},{9,1},{2,10},{10,2},{3,11},{11,3},{4,12},{12,4},... | collective-permute-start | bytes 2457608 | tf_op jit(solution)/shard_map/ppermute | solution.py:28
  69.7 21.1 %collective-permute-start.14 = (bf16[640,640]{1,0:T(8,128)(2,1)S(1)}, bf16[640,640]{1,0:T(8,128)(2,1)S(1)}, u32[]{:S(2)}, u32[]{:S(2)}) collective-permute-start(bf16[640,640]{1,0:T(8,128)(2,1)S(1)} %collective-permute-done.4.refs_3_), channel_id=1, source_target_pairs={{0,8},{8,0},{1,9},{9,1},{2,10},{10,2},{3,11},{11,3},{4,12},{12,4},... | collective-permute-start | bytes 2457608 | tf_op jit(solution)/shard_map/ppermute | solution.py:28
  76.0 14.8 %collective-permute-start.15 = (bf16[640,640]{1,0:T(8,128)(2,1)S(1)}, bf16[640,640]{1,0:T(8,128)(2,1)S(1)}, u32[]{:S(2)}, u32[]{:S(2)}) collective-permute-start(bf16[640,640]{1,0:T(8,128)(2,1)S(1)} %collective-permute-done.12.refs_2_), channel_id=1, source_target_pairs={{0,8},{8,0},{1,9},{9,1},{2,10},{10,2},{3,11},{11,3},{4,12},{12,4},... | collective-permute-start | bytes 2457608 | tf_op jit(solution)/shard_map/ppermute | solution.py:28
  77.4 13.5 %collective-permute-start.16 = (bf16[256,768]{1,0:T(8,128)(2,1)S(1)}, bf16[256,768]{1,0:T(8,128)(2,1)S(1)}, u32[]{:S(2)}, u32[]{:S(2)}) collective-permute-start(bf16[256,768]{1,0:T(8,128)(2,1)S(1)} %shard_map.70), channel_id=1, source_target_pairs={{0,16},{16,0},{1,17},{17,1},{2,18},{18,2},{3,19},{19,3},{4,20},{20... | collective-permute-start | bytes 1179656 | tf_op jit(solution)/shard_map/ppermute | solution.py:28
  82.1 16.8 %collective-permute-start.22 = (bf16[256,768]{1,0:T(8,128)(2,1)S(1)}, bf16[256,768]{1,0:T(8,128)(2,1)S(1)}, u32[]{:S(2)}, u32[]{:S(2)}) collective-permute-start(bf16[256,768]{1,0:T(8,128)(2,1)S(1)} %shard_map.71), channel_id=1, source_target_pairs={{0,16},{16,0},{1,17},{17,1},{2,18},{18,2},{3,19},{19,3},{4,20},{20... | collective-permute-start | bytes 1179656 | tf_op jit(solution)/shard_map/ppermute | solution.py:28
  91.5 11.1 %collective-permute-start.17 = (bf16[256,640]{1,0:T(8,128)(2,1)S(1)}, bf16[256,640]{1,0:T(8,128)(2,1)S(1)}, u32[]{:S(2)}, u32[]{:S(2)}) collective-permute-start(bf16[256,640]{1,0:T(8,128)(2,1)S(1)} %shard_map.74.refs_8_), channel_id=1, source_target_pairs={{0,3},{1,0},{2,1},{3,2},{4,7},{5,4},{6,5},{7,6},{8,11},{9,8},{10,9... | collective-permute-start | bytes 983048 | tf_op jit(solution)/shard_map/ppermute | solution.py:28
  94.5 11.4 %collective-permute-start.19 = (bf16[256,640]{1,0:T(8,128)(2,1)S(1)}, bf16[256,640]{1,0:T(8,128)(2,1)S(1)}, u32[]{:S(2)}, u32[]{:S(2)}) collective-permute-start(bf16[256,640]{1,0:T(8,128)(2,1)S(1)} %shard_map.74.refs_8_), channel_id=1, source_target_pairs={{0,1},{1,2},{2,3},{3,0},{4,5},{5,6},{6,7},{7,4},{8,9},{9,10},{10,1... | collective-permute-start | bytes 983048 | tf_op jit(solution)/shard_map/ppermute | solution.py:28
  99.5 19.7 %collective-permute-start.23 = (bf16[256,640]{1,0:T(8,128)(2,1)S(1)}, bf16[256,640]{1,0:T(8,128)(2,1)S(1)}, u32[]{:S(2)}, u32[]{:S(2)}) collective-permute-start(bf16[256,640]{1,0:T(8,128)(2,1)S(1)} %shard_map.77.refs_8_), channel_id=1, source_target_pairs={{0,3},{1,0},{2,1},{3,2},{4,7},{5,4},{6,5},{7,6},{8,11},{9,8},{10,9... | collective-permute-start | bytes 983048 | tf_op jit(solution)/shard_map/ppermute | solution.py:28
  102.5 17.0 %collective-permute-start.25 = (bf16[256,640]{1,0:T(8,128)(2,1)S(1)}, bf16[256,640]{1,0:T(8,128)(2,1)S(1)}, u32[]{:S(2)}, u32[]{:S(2)}) collective-permute-start(bf16[256,640]{1,0:T(8,128)(2,1)S(1)} %shard_map.77.refs_8_), channel_id=1, source_target_pairs={{0,1},{1,2},{2,3},{3,0},{4,5},{5,6},{6,7},{7,4},{8,9},{9,10},{10,1... | collective-permute-start | bytes 983048 | tf_op jit(solution)/shard_map/ppermute | solution.py:28
  102.6 10.3 %collective-permute-start.18 = (bf16[128,640]{1,0:T(8,128)(2,1)S(1)}, bf16[128,640]{1,0:T(8,128)(2,1)S(1)}, u32[]{:S(2)}, u32[]{:S(2)}) collective-permute-start(bf16[128,640]{1,0:T(8,128)(2,1)S(1)} %slice.24), channel_id=1, source_target_pairs={{0,3},{1,0},{2,1},{3,2},{4,7},{5,4},{6,5},{7,6},{8,11},{9,8},{10,9... | collective-permute-start | bytes 491528 | tf_op jit(solution)/shard_map/ppermute | solution.py:28
  105.9 10.4 %collective-permute-start.20 = (bf16[128,640]{1,0:T(8,128)(2,1)S(1)}, bf16[128,640]{1,0:T(8,128)(2,1)S(1)}, u32[]{:S(2)}, u32[]{:S(2)}) collective-permute-start(bf16[128,640]{1,0:T(8,128)(2,1)S(1)} %slice.25), channel_id=1, source_target_pairs={{0,1},{1,2},{2,3},{3,0},{4,5},{5,6},{6,7},{7,4},{8,9},{9,10},{10,1... | collective-permute-start | bytes 491528 | tf_op jit(solution)/shard_map/ppermute | solution.py:28
  117.8 13.2 %collective-permute-start.21 = (bf16[256,640]{1,0:T(8,128)(2,1)S(1)}, bf16[256,640]{1,0:T(8,128)(2,1)S(1)}, u32[]{:S(2)}, u32[]{:S(2)}) collective-permute-start(bf16[256,640]{1,0:T(8,128)(2,1)S(1)} %shard_map.76), channel_id=1, source_target_pairs={{0,4},{4,0},{1,5},{5,1},{2,6},{6,2},{3,7},{7,3},{8,12},{12,8},{9,1... | collective-permute-start | bytes 983048 | tf_op jit(solution)/shard_map/ppermute | solution.py:28
  119.2 5.4 %collective-permute-start.24 = (bf16[128,640]{1,0:T(8,128)(2,1)S(1)}, bf16[128,640]{1,0:T(8,128)(2,1)S(1)}, u32[]{:S(2)}, u32[]{:S(2)}) collective-permute-start(bf16[128,640]{1,0:T(8,128)(2,1)S(1)} %slice.26), channel_id=1, source_target_pairs={{0,3},{1,0},{2,1},{3,2},{4,7},{5,4},{6,5},{7,6},{8,11},{9,8},{10,9... | collective-permute-start | bytes 491528 | tf_op jit(solution)/shard_map/ppermute | solution.py:28
  119.6 6.6 %collective-permute-start.26 = (bf16[128,640]{1,0:T(8,128)(2,1)S(1)}, bf16[128,640]{1,0:T(8,128)(2,1)S(1)}, u32[]{:S(2)}, u32[]{:S(2)}) collective-permute-start(bf16[128,640]{1,0:T(8,128)(2,1)S(1)} %slice.27), channel_id=1, source_target_pairs={{0,1},{1,2},{2,3},{3,0},{4,5},{5,6},{6,7},{7,4},{8,9},{9,10},{10,1... | collective-permute-start | bytes 491528 | tf_op jit(solution)/shard_map/ppermute | solution.py:28
  127.5 7.2 %collective-permute-start.27 = (bf16[256,640]{1,0:T(8,128)(2,1)S(1)}, bf16[256,640]{1,0:T(8,128)(2,1)S(1)}, u32[]{:S(2)}, u32[]{:S(2)}) collective-permute-start(bf16[256,640]{1,0:T(8,128)(2,1)S(1)} %shard_map.79), channel_id=1, source_target_pairs={{0,4},{4,0},{1,5},{5,1},{2,6},{6,2},{3,7},{7,3},{8,12},{12,8},{9,1... | collective-permute-start | bytes 983048 | tf_op jit(solution)/shard_map/ppermute | solution.py:28
  (1 other events, 1.1 us)
where the time goes:
time: 138 us; the launch traced here: 136 us
  starting transfers between devices  46.6 us (34%)
  Pallas kernels  41 us (30%)
  waiting for transfers between devices  40.7 us (29%)
  local copies, waits for them, and re-layouts  6 us (4%)
    ppermute x28, starting transfers between devices, send(): lax.ppermute(value, axis, [(i, (i + step) % size) for i in range(size)])  46.6 us
    ppermute x28, waiting for transfers between devices, send(): lax.ppermute(value, axis, [(i, (i + step) % size) for i in range(size)])  40.7 us
    pallas_call x8, Pallas kernels, attention(): pl.pallas_call(functools.partial(attention_kernel, first, count_q, slots,...  33.2 us
    pallas_call x4, Pallas kernels, project(): pl.pallas_call(functools.partial(project_kernel, give), out_shape=jax.Sha...  5.46 us
  transfers between devices with their start and end apart: 28, of which 9 were waited for; matrix products, arithmetic and copies ran while one was open for 3% of the time, Pallas kernels for 30%

commit v1 on v0

--- a/solution.py
+++ b/solution.py
@@ -17,6 +17,7 @@
 BIG = 1e30
 SCALE = HEAD_DIM ** (-0.5) * math.log2(math.e)
 MIB = 1024 * 1024
+TALL = 256
 SLOT = {(0, 0): 0, (0, 1): 2, (1, 0): 4, (3, 0): 6, (1, 1): 8, (3, 1): 10, (2, 0): 12, (2, 1): 14}
 SMEM = pl.BlockSpec(memory_space=pltpu.SMEM)
 VMEM = pl.BlockSpec(memory_space=pltpu.VMEM)
@@ -88,73 +89,82 @@
 def attention_kernel(first, count_q, slots, state_at, last, k_mask, q_frame, *refs):
     q_parts, kv_parts = refs[:2], refs[2 : 2 + len(slots)]
     rest = refs[2 + len(slots) :]
-    queries = count_q * BLOCK
-    at = first * BLOCK
-    rows_at = pl.ds(at, queries)
     if state_at is not None:
         o_in, log_in = rest[:2]
         rest = rest[2:]
-        state_rows = pl.ds(at - state_at * BLOCK, queries)
     out = rest[0]
+    part, part_rows = first // 2, (first % 2) * BLOCK
+    if count_q > 2:
+        queries = rest[-1]
+        queries[:512, :] = q_parts[0][...]
+        queries[512:, :] = q_parts[1][...]
+        part_rows = 0
+    else:
+        queries = q_parts[part]
     hidden = jnp.concatenate(
         [k_mask[pl.ds(n * BLOCK, ref.shape[0]), :] for n, ref in zip(slots, kv_parts)], axis=0
     )
     keys = hidden.shape[0]
-    own_frame = q_frame[rows_at, :]
-    lane = lax.broadcasted_iota(jnp.int32, (queries, HEAD_DIM), 1)
+    tall = min(TALL, count_q * BLOCK)
+    lane = lax.broadcasted_iota(jnp.int32, (tall, HEAD_DIM), 1)
     ones = jnp.ones((keys, HEAD_DIM), jnp.bfloat16)
 
     def columns(h, offset=0):
         return pl.ds(offset + h * HEAD_DIM, HEAD_DIM)
 
-    def queries_of(h):
-        taken = []
-        for part, ref in enumerate(q_parts):
-            low, high = max(at - part * 512, 0), min(at + queries - part * 512, 512)
-            if low < high:
-                taken.append(ref[pl.ds(low, high - low), columns(h)])
-        return taken[0] if len(taken) == 1 else jnp.concatenate(taken, axis=0)
-
     def keys_of(h, offset):
         return jnp.concatenate([ref[:, columns(h, offset)] for ref in kv_parts], axis=0)
 
-    def score(h):
-        return lax.dot_general(
-            jnp.concatenate([queries_of(h), own_frame], axis=1),
-            jnp.concatenate([keys_of(h, 0), hidden], axis=1),
-            (((1,), (1,)), ((), ())),
-            preferred_element_type=jnp.float32,
-        )
-
-    def finish(h, acc, top, logs):
-        value, total = acc[:, :HEAD_DIM], acc[:, HEAD_DIM:]
-        top = jnp.broadcast_to(top * SCALE, (queries, HEAD_DIM))
+    def some_rows(n, carry):
+        def rows_from(start):
+            return pl.ds(pl.multiple_of(start + n * tall, BLOCK), tall)
+
+        rows = rows_from(0)
+        q_rows = rows_from(part_rows)
+        own_frame = q_frame[rows_from(first * BLOCK), :]
         if state_at is not None:
-            log = jnp.broadcast_to(log_in[state_rows, pl.ds(h, 1)], (queries, HEAD_DIM))
-            both = jnp.maximum(log, top)
-            new, old = jnp.exp2(top - both), jnp.exp2(log - both)
-            value = value * new + o_in[state_rows, columns(h)] * old
-            total = total * new + old
-            top = both
-        out[:, columns(h)] = (value / total).astype(out.dtype)
-        return jnp.where(lane == h, top + jnp.log2(total), logs)
-
-    logs = jnp.zeros((queries, HEAD_DIM), jnp.float32)
-    scores, held = score(0), None
-    for h in range(HEADS):
-        ahead = score(h + 1) if h + 1 < HEADS else None
-        top = jnp.max(scores, axis=1, keepdims=True)
-        expo = jnp.exp2((scores - top) * SCALE).astype(jnp.bfloat16)
-        values = jnp.concatenate([keys_of(h, WIDTH), ones], axis=1)
-        acc = jnp.dot(expo, values, preferred_element_type=jnp.float32)
-        if held is not None:
-            logs = finish(h - 1, *held, logs)
-        held, scores = (acc, top), ahead
-    logs = finish(HEADS - 1, *held, logs)
-    if last:
-        out[:, pl.ds(WIDTH, HEAD_DIM)] = three_pieces(logs)
-    else:
-        rest[1][...] = logs
+            state_rows = rows_from((first - state_at) * BLOCK)
+
+        def score(h):
+            return lax.dot_general(
+                jnp.concatenate([queries[q_rows, columns(h)], own_frame], axis=1),
+                jnp.concatenate([keys_of(h, 0), hidden], axis=1),
+                (((1,), (1,)), ((), ())),
+                preferred_element_type=jnp.float32,
+            )
+
+        def finish(h, acc, top, logs):
+            value, total = acc[:, :HEAD_DIM], acc[:, HEAD_DIM:]
+            top = jnp.broadcast_to(top * SCALE, (tall, HEAD_DIM))
+            if state_at is not None:
+                log = jnp.broadcast_to(log_in[state_rows, pl.ds(h, 1)], (tall, HEAD_DIM))
+                both = jnp.maximum(log, top)
+                new, old = jnp.exp2(top - both), jnp.exp2(log - both)
+                value = value * new + o_in[state_rows, columns(h)] * old
+                total = total * new + old
+                top = both
+            out[rows, columns(h)] = (value / total).astype(out.dtype)
+            return jnp.where(lane == h, top + jnp.log2(total), logs)
+
+        logs = jnp.zeros((tall, HEAD_DIM), jnp.float32)
+        scores, held = score(0), None
+        for h in range(HEADS):
+            ahead = score(h + 1) if h + 1 < HEADS else None
+            top = jnp.max(scores, axis=1, keepdims=True)
+            expo = jnp.exp2((scores - top) * SCALE).astype(jnp.bfloat16)
+            values = jnp.concatenate([keys_of(h, WIDTH), ones], axis=1)
+            acc = jnp.dot(expo, values, preferred_element_type=jnp.float32)
+            if held is not None:
+                logs = finish(h - 1, *held, logs)
+            held, scores = (acc, top), ahead
+        logs = finish(HEADS - 1, *held, logs)
+        if last:
+            out[rows, pl.ds(WIDTH, HEAD_DIM)] = three_pieces(logs)
+        else:
+            rest[1][rows, :] = logs
+        return carry
+
+    lax.fori_loop(0, count_q * BLOCK // tall, some_rows, 0)
 
 
 def attention(blocks, tabled, q_parts, kv_parts, state=(), state_at=0, last=False):
@@ -175,6 +185,7 @@
         out_shape=out_shape,
         in_specs=[VMEM] * (4 + len(kv_parts) + len(state)),
         out_specs=(VMEM,) * len(out_shape),
+        scratch_shapes=[pltpu.VMEM((rows, WIDTH), jnp.bfloat16)] if count_q > 2 else [],
         compiler_params=pltpu.CompilerParams(vmem_limit_bytes=30 * MIB),
         cost_estimate=SMALL,
     )(*tabled, *q_parts, *(part for _, part in kv_parts), *state)

time: 138 us -> 125 us (0.906); the launches traced: 136 us -> 125 us
  starting transfers between devices: 46.6 us -> 34.3 us
  Pallas kernels: 41 us -> 44.9 us
  waiting for transfers between devices: 40.7 us -> 37.9 us
    ppermute x28, starting transfers between devices: 46.6 us -> 34.3 us  [send(): lax.ppermute(value, axis, [(i, (i + step) % size) for i in range(size)])]
    pallas_call x8, Pallas kernels: 33.2 us -> 37.3 us  [attention(): pl.pallas_call(functools.partial(attention_kernel, first, count_q, slots,...]
    ppermute x28, waiting for transfers between devices: 40.7 us -> 37.9 us  [send(): lax.ppermute(value, axis, [(i, (i + step) % size) for i in range(size)])]
  transfers between devices with their start and end apart: 28 -> 28, of which waited for: 9 -> 9; matrix products, arithmetic and copies ran while one was open for 3% -> 3% of each run, Pallas kernels for 30% -> 36%
where the time goes in v1:
time: 125 us
  Pallas kernels  44.9 us (36%)
  waiting for transfers between devices  37.9 us (30%)
  starting transfers between devices  34.3 us (27%)
  local copies, waits for them, and re-layouts  6 us (5%)
    ppermute x28, waiting for transfers between devices, send(): lax.ppermute(value, axis, [(i, (i + step) % size) for i in range(size)])  37.9 us
    pallas_call x8, Pallas kernels, attention(): pl.pallas_call(functools.partial(attention_kernel, first, count_q, slots,...  37.3 us
    ppermute x28, starting transfers between devices, send(): lax.ppermute(value, axis, [(i, (i + step) % size) for i in range(size)])  34.3 us
    pallas_call x4, Pallas kernels, project(): pl.pallas_call(functools.partial(project_kernel, give), out_shape=jax.Sha...  5.3 us
    dynamic_slice x1, local copies, waits for them, and re-layouts, columns(): lax.dynamic_slice_in_dim(w_out, (zl * 4 + (x_at + distance) % 4) * 640, 6...  2.58 us
  transfers between devices with their start and end apart: 28, of which 9 were waited for; matrix products, arithmetic and copies ran while one was open for 3% of the time, Pallas kernels for 36%

profile of v1, /device:TPU:0, one launch (start us, length us, event | category | flops | bytes accessed | tf_op | source)
XLA Modules:
  0.0 124.5 jit_solution(2947680184330642646)
XLA Ops:
  2.4 3.2 %collective-permute-start = (bf16[512,1280]{1,0:T(8,128)(2,1)S(1)}, bf16[512,1280]{1,0:T(8,128)(2,1)S(1)}, u32[]{:S(2)}, u32[]{:S(2)}) collective-permute-start(bf16[512,1280]{1,0:T(8,128)(2,1)S(1)} %shard_map.64.refs_2_), channel_id=1, source_target_pairs={{0,96},{32,0},{64,32},{96,64},{1,97},{33,1},{65,33},{97,65},{2,98}... | collective-permute-start | bytes 3932168 | tf_op jit(solution)/shard_map/ppermute | solution.py:29
  5.6 2.6 %constant_dynamic-slice_fusion = (bf16[640,640]{1,0:T(8,128)(2,1)S(1)}, bf16[640,640]{1,0:T(8,128)(2,1)S(1)}, bf16[640,640]{1,0:T(8,128)(2,1)S(1)}, bf16[640,640]{1,0:T(8,128)(2,1)S(1)}, bf16[640,640]{1,0:T(8,128)(2,1)S(1)}) fusion(bf16[640,5120]{1,0:T(8,128)(2,1)} %param.11, s32[]{:T(128)S(6)} %select_n.44, s32[]{:T(128)S(6)} %select_n.41, s32[]{:T(128)S(6)} %select_n.39, ...), kind=kLoop, calls=%fused_computation.3 | loop fusion | bytes 8192020 | tf_op jit(solution)/shard_map/dynamic_slice | solution.py:300
  8.2 2.8 %collective-permute-start.3 = (bf16[640,640]{1,0:T(8,128)(2,1)S(1)}, bf16[640,640]{1,0:T(8,128)(2,1)S(1)}, u32[]{:S(2)}, u32[]{:S(2)}) collective-permute-start(bf16[640,640]{1,0:T(8,128)(2,1)S(1)} %get-tuple-element.43), channel_id=1, source_target_pairs={{0,3},{1,0},{2,1},{3,2},{4,7},{5,4},{6,5},{7,6},{8,11},{9,8},{10,9... | collective-permute-start | bytes 2457608 | tf_op jit(solution)/shard_map/ppermute | solution.py:29
  11.0 3.9 %collective-permute-start.5 = (bf16[512,640]{1,0:T(8,128)(2,1)S(1)}, bf16[512,640]{1,0:T(8,128)(2,1)S(1)}, u32[]{:S(2)}, u32[]{:S(2)}) collective-permute-start(bf16[512,640]{1,0:T(8,128)(2,1)S(1)} %copy-done), channel_id=1, source_target_pairs={{0,16},{16,0},{1,17},{17,1},{2,18},{18,2},{3,19},{19,3},{4,20},{20... | collective-permute-start | bytes 1966088 | tf_op jit(solution)/shard_map/ppermute | solution.py:29
  16.0 13.7 %collective-permute-done.5.refs_0_ = bf16[512,640]{1,0:T(8,128)(2,1)S(1)} collective-permute-done((bf16[512,640]{1,0:T(8,128)(2,1)S(1)}, bf16[512,640]{1,0:T(8,128)(2,1)S(1)}, u32[]{:S(2)}, u32[]{:S(2)}) %collective-permute-start.5) | collective-permute-done | bytes 655392 | tf_op jit(solution)/shard_map/ppermute | solution.py:29
  29.7 9.1 %shard_map.66 = (f32[1024,640]{1,0:T(8,128)S(1)}, f32[1024,128]{1,0:T(8,128)S(1)}) custom-call(bf16[4096,128]{1,0:T(8,128)(2,1)S(1)} %get-tuple-element.45.k_mask, bf16[1024,128]{1,0:T(8,128)(2,1)S(1)} %get-tuple-element.46.q_frame, bf16[512,640]{1,0:T(8,128)(2,1)S(1)} %collective-permute-done.5.refs_0_, bf16[512,640]{1,0:T(8,128)(2,1)S(1)} %copy-done, ...), custom_call_target="tpu_custom_call" | custom-call | flops 1024 | bytes 1024 | tf_op jit(solution)/shard_map/pallas_call | solution.py:181
  40.6 3.0 %collective-permute-start.6 = (bf16[256,1280]{1,0:T(8,128)(2,1)S(1)}, bf16[256,1280]{1,0:T(8,128)(2,1)S(1)}, u32[]{:S(2)}, u32[]{:S(2)}) collective-permute-start(bf16[256,1280]{1,0:T(8,128)(2,1)S(1)} %slice.18), channel_id=1, source_target_pairs={{0,96},{32,0},{64,32},{96,64},{1,97},{33,1},{65,33},{97,65},{2,98}... | collective-permute-start | bytes 1966088 | tf_op jit(solution)/shard_map/ppermute | solution.py:29
  43.6 2.0 %collective-permute-start.12 = (bf16[640,640]{1,0:T(8,128)(2,1)S(1)}, bf16[640,640]{1,0:T(8,128)(2,1)S(1)}, u32[]{:S(2)}, u32[]{:S(2)}) collective-permute-start(bf16[640,640]{1,0:T(8,128)(2,1)S(1)} %get-tuple-element.60), channel_id=1, source_target_pairs={{0,2},{1,3},{2,0},{3,1},{4,6},{5,7},{6,4},{7,5},{8,10},{9,11},{10,... | collective-permute-start | bytes 2457608 | tf_op jit(solution)/shard_map/ppermute | solution.py:29
  45.6 9.8 %shard_map.67 = (f32[1024,640]{1,0:T(8,128)S(1)}, f32[1024,128]{1,0:T(8,128)S(1)}) custom-call(bf16[4096,128]{1,0:T(8,128)(2,1)S(1)} %get-tuple-element.45.k_mask, bf16[1024,128]{1,0:T(8,128)(2,1)S(1)} %get-tuple-element.46.q_frame, bf16[512,640]{1,0:T(8,128)(2,1)S(1)} %collective-permute-done.5.refs_0_, bf16[512,640]{1,0:T(8,128)(2,1)S(1)} %copy-done, ...), custom_call_target="tpu_custom_call" | custom-call | flops 1024 | bytes 1024 | tf_op jit(solution)/shard_map/pallas_call | solution.py:181
  55.4 4.2 %shard_map.68 = (f32[512,640]{1,0:T(8,128)S(1)}, f32[512,128]{1,0:T(8,128)S(1)}) custom-call(bf16[4096,128]{1,0:T(8,128)(2,1)S(1)} %get-tuple-element.45.k_mask, bf16[1024,128]{1,0:T(8,128)(2,1)S(1)} %get-tuple-element.46.q_frame, bf16[512,640]{1,0:T(8,128)(2,1)S(1)} %collective-permute-done.5.refs_0_, bf16[512,640]{1,0:T(8,128)(2,1)S(1)} %copy-done, ...), custom_call_target="tpu_custom_call" | custom-call | flops 1024 | bytes 1024 | tf_op jit(solution)/shard_map/pallas_call | solution.py:181
  59.7 1.5 %collective-permute-done.7.refs_3_ = bf16[256,1280]{1,0:T(8,128)(2,1)S(1)} collective-permute-done((bf16[256,1280]{1,0:T(8,128)(2,1)S(1)}, bf16[256,1280]{1,0:T(8,128)(2,1)S(1)}, u32[]{:S(2)}, u32[]{:S(2)}) %collective-permute-start.7) | collective-permute-done | bytes 655392 | tf_op jit(solution)/shard_map/ppermute | solution.py:29
  62.3 2.7 %shard_map.69 = (f32[512,640]{1,0:T(8,128)S(1)}, f32[512,128]{1,0:T(8,128)S(1)}) custom-call(bf16[4096,128]{1,0:T(8,128)(2,1)S(1)} %get-tuple-element.45.k_mask, bf16[1024,128]{1,0:T(8,128)(2,1)S(1)} %get-tuple-element.46.q_frame, bf16[512,640]{1,0:T(8,128)(2,1)S(1)} %collective-permute-done.5.refs_0_, bf16[512,640]{1,0:T(8,128)(2,1)S(1)} %copy-done, ...), custom_call_target="tpu_custom_call" | custom-call | flops 1024 | bytes 1024 | tf_op jit(solution)/shard_map/pallas_call | solution.py:181
  65.1 1.4 %shard_map.70 = bf16[256,768]{1,0:T(8,128)(2,1)S(1)} custom-call(bf16[4096,128]{1,0:T(8,128)(2,1)S(1)} %get-tuple-element.45.k_mask, bf16[1024,128]{1,0:T(8,128)(2,1)S(1)} %get-tuple-element.46.q_frame, bf16[512,640]{1,0:T(8,128)(2,1)S(1)} %collective-permute-done.5.refs_0_, bf16[512,640]{1,0:T(8,128)(2,1)S(1)} %copy-done, ...), custom_call_target="tpu_custom_call" | custom-call | flops 1024 | bytes 1024 | tf_op jit(solution)/shard_map/pallas_call | solution.py:181
  66.5 3.3 %collective-permute-start.16 = (bf16[256,768]{1,0:T(8,128)(2,1)S(1)}, bf16[256,768]{1,0:T(8,128)(2,1)S(1)}, u32[]{:S(2)}, u32[]{:S(2)}) collective-permute-start(bf16[256,768]{1,0:T(8,128)(2,1)S(1)} %shard_map.70), channel_id=1, source_target_pairs={{0,16},{16,0},{1,17},{17,1},{2,18},{18,2},{3,19},{19,3},{4,20},{20... | collective-permute-start | bytes 1179656 | tf_op jit(solution)/shard_map/ppermute | solution.py:29
  69.8 1.4 %shard_map.71 = bf16[256,768]{1,0:T(8,128)(2,1)S(1)} custom-call(bf16[4096,128]{1,0:T(8,128)(2,1)S(1)} %get-tuple-element.45.k_mask, bf16[1024,128]{1,0:T(8,128)(2,1)S(1)} %get-tuple-element.46.q_frame, bf16[512,640]{1,0:T(8,128)(2,1)S(1)} %collective-permute-done.5.refs_0_, bf16[512,640]{1,0:T(8,128)(2,1)S(1)} %copy-done, ...), custom_call_target="tpu_custom_call" | custom-call | flops 1024 | bytes 1024 | tf_op jit(solution)/shard_map/pallas_call | solution.py:181
  71.6 4.2 %shard_map.72 = (f32[512,640]{1,0:T(8,128)S(1)}, f32[512,128]{1,0:T(8,128)S(1)}) custom-call(bf16[4096,128]{1,0:T(8,128)(2,1)S(1)} %get-tuple-element.45.k_mask, bf16[1024,128]{1,0:T(8,128)(2,1)S(1)} %get-tuple-element.46.q_frame, bf16[512,640]{1,0:T(8,128)(2,1)S(1)} %collective-permute-done.5.refs_0_, bf16[512,640]{1,0:T(8,128)(2,1)S(1)} %copy-done, ...), custom_call_target="tpu_custom_call" | custom-call | flops 1024 | bytes 1024 | tf_op jit(solution)/shard_map/pallas_call | solution.py:181
  75.8 4.4 %shard_map.73.mine = bf16[512,768]{1,0:T(8,128)(2,1)S(1)} custom-call(bf16[4096,128]{1,0:T(8,128)(2,1)S(1)} %get-tuple-element.45.k_mask, bf16[1024,128]{1,0:T(8,128)(2,1)S(1)} %get-tuple-element.46.q_frame, bf16[512,640]{1,0:T(8,128)(2,1)S(1)} %collective-permute-done.5.refs_0_, bf16[512,640]{1,0:T(8,128)(2,1)S(1)} %copy-done, ...), custom_call_target="tpu_custom_call" | custom-call | flops 1024 | bytes 1024 | tf_op jit(solution)/shard_map/pallas_call | solution.py:181
  80.9 3.0 %collective-permute-start.17 = (bf16[256,640]{1,0:T(8,128)(2,1)S(1)}, bf16[256,640]{1,0:T(8,128)(2,1)S(1)}, u32[]{:S(2)}, u32[]{:S(2)}) collective-permute-start(bf16[256,640]{1,0:T(8,128)(2,1)S(1)} %shard_map.74.refs_8_), channel_id=1, source_target_pairs={{0,3},{1,0},{2,1},{3,2},{4,7},{5,4},{6,5},{7,6},{8,11},{9,8},{10,9... | collective-permute-start | bytes 983048 | tf_op jit(solution)/shard_map/ppermute | solution.py:29
  83.9 4.1 %collective-permute-done.22.theirs = bf16[256,768]{1,0:T(8,128)(2,1)S(1)} collective-permute-done((bf16[256,768]{1,0:T(8,128)(2,1)S(1)}, bf16[256,768]{1,0:T(8,128)(2,1)S(1)}, u32[]{:S(2)}, u32[]{:S(2)}) %collective-permute-start.22) | collective-permute-done | bytes 393248 | tf_op jit(solution)/shard_map/ppermute | solution.py:29
  88.6 3.0 %collective-permute-start.23 = (bf16[256,640]{1,0:T(8,128)(2,1)S(1)}, bf16[256,640]{1,0:T(8,128)(2,1)S(1)}, u32[]{:S(2)}, u32[]{:S(2)}) collective-permute-start(bf16[256,640]{1,0:T(8,128)(2,1)S(1)} %shard_map.77.refs_8_), channel_id=1, source_target_pairs={{0,3},{1,0},{2,1},{3,2},{4,7},{5,4},{6,5},{7,6},{8,11},{9,8},{10,9... | collective-permute-start | bytes 983048 | tf_op jit(solution)/shard_map/ppermute | solution.py:29
  91.6 3.3 %collective-permute-start.18 = (bf16[128,640]{1,0:T(8,128)(2,1)S(1)}, bf16[128,640]{1,0:T(8,128)(2,1)S(1)}, u32[]{:S(2)}, u32[]{:S(2)}) collective-permute-start(bf16[128,640]{1,0:T(8,128)(2,1)S(1)} %slice.24), channel_id=1, source_target_pairs={{0,3},{1,0},{2,1},{3,2},{4,7},{5,4},{6,5},{7,6},{8,11},{9,8},{10,9... | collective-permute-start | bytes 491528 | tf_op jit(solution)/shard_map/ppermute | solution.py:29
  95.3 6.7 %collective-permute-done.18.refs_10_ = bf16[128,640]{1,0:T(8,128)(2,1)S(1)} collective-permute-done((bf16[128,640]{1,0:T(8,128)(2,1)S(1)}, bf16[128,640]{1,0:T(8,128)(2,1)S(1)}, u32[]{:S(2)}, u32[]{:S(2)}) %collective-permute-start.18) | collective-permute-done | bytes 163872 | tf_op jit(solution)/shard_map/ppermute | solution.py:29
  102.0 3.4 %collective-permute-done.20.refs_11_ = bf16[128,640]{1,0:T(8,128)(2,1)S(1)} collective-permute-done((bf16[128,640]{1,0:T(8,128)(2,1)S(1)}, bf16[128,640]{1,0:T(8,128)(2,1)S(1)}, u32[]{:S(2)}, u32[]{:S(2)}) %collective-permute-start.20) | collective-permute-done | bytes 163872 | tf_op jit(solution)/shard_map/ppermute | solution.py:29
  105.4 1.3 %shard_map.76 = bf16[256,640]{1,0:T(8,128)(2,1)S(1)} custom-call(bf16[640,640]{1,0:T(8,128)(2,1)S(1)} %get-tuple-element.84.refs_0_, bf16[640,640]{1,0:T(8,128)(2,1)S(1)} %collective-permute-done.3.refs_1_, bf16[640,640]{1,0:T(8,128)(2,1)S(1)} %collective-permute-done.12.refs_2_, bf16[640,640]{1,0:T(8,128)(2,1)S(1)} %collective-permute-done.4.refs_3_, ...), custom_call_target="tpu_custom_call" | custom-call | flops 1024 | bytes 1024 | tf_op jit(solution)/shard_map/pallas_call | solution.py:281
  106.7 1.4 %collective-permute-start.21 = (bf16[256,640]{1,0:T(8,128)(2,1)S(1)}, bf16[256,640]{1,0:T(8,128)(2,1)S(1)}, u32[]{:S(2)}, u32[]{:S(2)}) collective-permute-start(bf16[256,640]{1,0:T(8,128)(2,1)S(1)} %shard_map.76), channel_id=1, source_target_pairs={{0,4},{4,0},{1,5},{5,1},{2,6},{6,2},{3,7},{7,3},{8,12},{12,8},{9,1... | collective-permute-start | bytes 983048 | tf_op jit(solution)/shard_map/ppermute | solution.py:29
  108.5 1.8 %collective-permute-start.26 = (bf16[128,640]{1,0:T(8,128)(2,1)S(1)}, bf16[128,640]{1,0:T(8,128)(2,1)S(1)}, u32[]{:S(2)}, u32[]{:S(2)}) collective-permute-start(bf16[128,640]{1,0:T(8,128)(2,1)S(1)} %slice.27), channel_id=1, source_target_pairs={{0,1},{1,2},{2,3},{3,0},{4,5},{5,6},{6,7},{7,4},{8,9},{9,10},{10,1... | collective-permute-start | bytes 491528 | tf_op jit(solution)/shard_map/ppermute | solution.py:29
  110.3 3.2 %collective-permute-done.24.refs_10_ = bf16[128,640]{1,0:T(8,128)(2,1)S(1)} collective-permute-done((bf16[128,640]{1,0:T(8,128)(2,1)S(1)}, bf16[128,640]{1,0:T(8,128)(2,1)S(1)}, u32[]{:S(2)}, u32[]{:S(2)}) %collective-permute-start.24) | collective-permute-done | bytes 163872 | tf_op jit(solution)/shard_map/ppermute | solution.py:29
  113.5 1.6 %collective-permute-done.26.refs_11_ = bf16[128,640]{1,0:T(8,128)(2,1)S(1)} collective-permute-done((bf16[128,640]{1,0:T(8,128)(2,1)S(1)}, bf16[128,640]{1,0:T(8,128)(2,1)S(1)}, u32[]{:S(2)}, u32[]{:S(2)}) %collective-permute-start.26) | collective-permute-done | bytes 163872 | tf_op jit(solution)/shard_map/ppermute | solution.py:29
  115.1 1.3 %shard_map.79 = bf16[256,640]{1,0:T(8,128)(2,1)S(1)} custom-call(bf16[640,640]{1,0:T(8,128)(2,1)S(1)} %get-tuple-element.84.refs_0_, bf16[640,640]{1,0:T(8,128)(2,1)S(1)} %collective-permute-done.3.refs_1_, bf16[640,640]{1,0:T(8,128)(2,1)S(1)} %collective-permute-done.12.refs_2_, bf16[640,640]{1,0:T(8,128)(2,1)S(1)} %collective-permute-done.4.refs_3_, ...), custom_call_target="tpu_custom_call" | custom-call | flops 1024 | bytes 1024 | tf_op jit(solution)/shard_map/pallas_call | solution.py:281
  117.2 1.3 %shard_map.75 = f32[256,640]{1,0:T(8,128)S(1)} custom-call(bf16[640,640]{1,0:T(8,128)(2,1)S(1)} %get-tuple-element.84.refs_0_, bf16[640,640]{1,0:T(8,128)(2,1)S(1)} %collective-permute-done.3.refs_1_, bf16[640,640]{1,0:T(8,128)(2,1)S(1)} %collective-permute-done.12.refs_2_, bf16[640,640]{1,0:T(8,128)(2,1)S(1)} %collective-permute-done.4.refs_3_, ...), custom_call_target="tpu_custom_call" | custom-call | flops 1024 | bytes 1024 | tf_op jit(solution)/shard_map/pallas_call | solution.py:281
  118.6 1.3 %shard_map.78 = f32[256,640]{1,0:T(8,128)S(1)} custom-call(bf16[640,640]{1,0:T(8,128)(2,1)S(1)} %get-tuple-element.84.refs_0_, bf16[640,640]{1,0:T(8,128)(2,1)S(1)} %collective-permute-done.3.refs_1_, bf16[640,640]{1,0:T(8,128)(2,1)S(1)} %collective-permute-done.12.refs_2_, bf16[640,640]{1,0:T(8,128)(2,1)S(1)} %collective-permute-done.4.refs_3_, ...), custom_call_target="tpu_custom_call" | custom-call | flops 1024 | bytes 1024 | tf_op jit(solution)/shard_map/pallas_call | solution.py:281
  120.0 3.6 %collective-permute-done.27 = bf16[256,640]{1,0:T(8,128)(2,1)S(1)} collective-permute-done((bf16[256,640]{1,0:T(8,128)(2,1)S(1)}, bf16[256,640]{1,0:T(8,128)(2,1)S(1)}, u32[]{:S(2)}, u32[]{:S(2)}) %collective-permute-start.27) | collective-permute-done | bytes 327712 | tf_op jit(solution)/shard_map/ppermute | solution.py:29
  (60 shorter events, 10.5 us)
Async XLA Ops:
  1.1 1.1 copy-start.2
  2.3 5.9 %collective-permute-start.2 = (bf16[512,1280]{1,0:T(8,128)(2,1)S(1)}, bf16[512,1280]{1,0:T(8,128)(2,1)}, u32[]{:S(2)}, u32[]{:S(2)}) collective-permute-start(bf16[512,1280]{1,0:T(8,128)(2,1)S(1)} %shard_map.64.refs_2_), channel_id=1, source_target_pairs={{0,8},{8,0},{1,9},{9,1},{2,10},{10,2},{3,11},{11,3},{4,12},{12,4},... | collective-permute-start | bytes 3932168 | tf_op jit(solution)/shard_map/ppermute | solution.py:29
  2.4 36.3 %collective-permute-start = (bf16[512,1280]{1,0:T(8,128)(2,1)S(1)}, bf16[512,1280]{1,0:T(8,128)(2,1)S(1)}, u32[]{:S(2)}, u32[]{:S(2)}) collective-permute-start(bf16[512,1280]{1,0:T(8,128)(2,1)S(1)} %shard_map.64.refs_2_), channel_id=1, source_target_pairs={{0,96},{32,0},{64,32},{96,64},{1,97},{33,1},{65,33},{97,65},{2,98}... | collective-permute-start | bytes 3932168 | tf_op jit(solution)/shard_map/ppermute | solution.py:29
  5.6 33.2 %collective-permute-start.1 = (bf16[512,1280]{1,0:T(8,128)(2,1)S(1)}, bf16[512,1280]{1,0:T(8,128)(2,1)}, u32[]{:S(2)}, u32[]{:S(2)}) collective-permute-start(bf16[512,1280]{1,0:T(8,128)(2,1)S(1)} %shard_map.64.refs_2_), channel_id=1, source_target_pairs={{0,32},{32,64},{64,96},{96,0},{1,33},{33,65},{65,97},{97,1},{2,34}... | collective-permute-start | bytes 3932168 | tf_op jit(solution)/shard_map/ppermute | solution.py:29
  5.6 5.4 %copy-start = (bf16[512,640]{1,0:T(8,128)(2,1)S(1)}, bf16[512,640]{1,0:T(8,128)(2,1)}, u32[]{:S(2)}) copy-start(bf16[512,640]{1,0:T(8,128)(2,1)} %refs_1_.15) | copy-start | bytes 1966084
  5.6 9.3 %copy-start.3 = (s32[8192]{0:T(1024)S(1)}, s32[8192]{0:T(1024)}, u32[]{:S(2)}) copy-start(s32[8192]{0:T(1024)} %param.9) | copy-start | bytes 98308
  5.6 9.3 %copy-start.4 = (s32[32]{0:T(128)S(1)}, s32[32]{0:T(128)}, u32[]{:S(2)}) copy-start(s32[32]{0:T(128)} %order_ref.1) | copy-start | bytes 388
  8.2 30.6 %collective-permute-start.3 = (bf16[640,640]{1,0:T(8,128)(2,1)S(1)}, bf16[640,640]{1,0:T(8,128)(2,1)S(1)}, u32[]{:S(2)}, u32[]{:S(2)}) collective-permute-start(bf16[640,640]{1,0:T(8,128)(2,1)S(1)} %get-tuple-element.43), channel_id=1, source_target_pairs={{0,3},{1,0},{2,1},{3,2},{4,7},{5,4},{6,5},{7,6},{8,11},{9,8},{10,9... | collective-permute-start | bytes 2457608 | tf_op jit(solution)/shard_map/ppermute | solution.py:29
  11.0 27.8 %collective-permute-start.4 = (bf16[640,640]{1,0:T(8,128)(2,1)S(1)}, bf16[640,640]{1,0:T(8,128)(2,1)S(1)}, u32[]{:S(2)}, u32[]{:S(2)}) collective-permute-start(bf16[640,640]{1,0:T(8,128)(2,1)S(1)} %get-tuple-element.44), channel_id=1, source_target_pairs={{0,1},{1,2},{2,3},{3,0},{4,5},{5,6},{6,7},{7,4},{8,9},{9,10},{10,1... | collective-permute-start | bytes 2457608 | tf_op jit(solution)/shard_map/ppermute | solution.py:29
  11.0 18.7 %collective-permute-start.5 = (bf16[512,640]{1,0:T(8,128)(2,1)S(1)}, bf16[512,640]{1,0:T(8,128)(2,1)S(1)}, u32[]{:S(2)}, u32[]{:S(2)}) collective-permute-start(bf16[512,640]{1,0:T(8,128)(2,1)S(1)} %copy-done), channel_id=1, source_target_pairs={{0,16},{16,0},{1,17},{17,1},{2,18},{18,2},{3,19},{19,3},{4,20},{20... | collective-permute-start | bytes 1966088 | tf_op jit(solution)/shard_map/ppermute | solution.py:29
  38.8 16.6 %collective-permute-start.8 = (bf16[512,1280]{1,0:T(8,128)(2,1)S(1)}, bf16[512,1280]{1,0:T(8,128)(2,1)S(1)}, u32[]{:S(2)}, u32[]{:S(2)}) collective-permute-start(bf16[512,1280]{1,0:T(8,128)(2,1)S(1)} %collective-permute-done.refs_2_), channel_id=1, source_target_pairs={{0,8},{8,0},{1,9},{9,1},{2,10},{10,2},{3,11},{11,3},{4,12},{12,4},... | collective-permute-start | bytes 3932168 | tf_op jit(solution)/shard_map/ppermute | solution.py:29
  38.9 16.6 %collective-permute-start.9 = (bf16[512,1280]{1,0:T(8,128)(2,1)}, bf16[512,1280]{1,0:T(8,128)(2,1)S(1)}, u32[]{:S(2)}, u32[]{:S(2)}) collective-permute-start(bf16[512,1280]{1,0:T(8,128)(2,1)} %collective-permute-done.1.refs_3_), channel_id=1, source_target_pairs={{0,8},{8,0},{1,9},{9,1},{2,10},{10,2},{3,11},{11,3},{4,12},{12,4},... | collective-permute-start | bytes 3932168 | tf_op jit(solution)/shard_map/ppermute | solution.py:29
  40.6 19.1 %collective-permute-start.6 = (bf16[256,1280]{1,0:T(8,128)(2,1)S(1)}, bf16[256,1280]{1,0:T(8,128)(2,1)S(1)}, u32[]{:S(2)}, u32[]{:S(2)}) collective-permute-start(bf16[256,1280]{1,0:T(8,128)(2,1)S(1)} %slice.18), channel_id=1, source_target_pairs={{0,96},{32,0},{64,32},{96,64},{1,97},{33,1},{65,33},{97,65},{2,98}... | collective-permute-start | bytes 1966088 | tf_op jit(solution)/shard_map/ppermute | solution.py:29
  43.6 17.7 %collective-permute-start.7 = (bf16[256,1280]{1,0:T(8,128)(2,1)S(1)}, bf16[256,1280]{1,0:T(8,128)(2,1)S(1)}, u32[]{:S(2)}, u32[]{:S(2)}) collective-permute-start(bf16[256,1280]{1,0:T(8,128)(2,1)S(1)} %slice.19), channel_id=1, source_target_pairs={{0,32},{32,64},{64,96},{96,0},{1,33},{33,65},{65,97},{97,1},{2,34}... | collective-permute-start | bytes 1966088 | tf_op jit(solution)/shard_map/ppermute | solution.py:29
  43.6 21.5 %collective-permute-start.12 = (bf16[640,640]{1,0:T(8,128)(2,1)S(1)}, bf16[640,640]{1,0:T(8,128)(2,1)S(1)}, u32[]{:S(2)}, u32[]{:S(2)}) collective-permute-start(bf16[640,640]{1,0:T(8,128)(2,1)S(1)} %get-tuple-element.60), channel_id=1, source_target_pairs={{0,2},{1,3},{2,0},{3,1},{4,6},{5,7},{6,4},{7,5},{8,10},{9,11},{10,... | collective-permute-start | bytes 2457608 | tf_op jit(solution)/shard_map/ppermute | solution.py:29
  61.2 3.8 %collective-permute-start.10 = (bf16[256,1280]{1,0:T(8,128)(2,1)S(1)}, bf16[256,1280]{1,0:T(8,128)(2,1)S(1)}, u32[]{:S(2)}, u32[]{:S(2)}) collective-permute-start(bf16[256,1280]{1,0:T(8,128)(2,1)S(1)} %collective-permute-done.6.refs_2_), channel_id=1, source_target_pairs={{0,8},{8,0},{1,9},{9,1},{2,10},{10,2},{3,11},{11,3},{4,12},{12,4},... | collective-permute-start | bytes 1966088 | tf_op jit(solution)/shard_map/ppermute | solution.py:29
  61.2 3.8 %collective-permute-start.11 = (bf16[256,1280]{1,0:T(8,128)(2,1)S(1)}, bf16[256,1280]{1,0:T(8,128)(2,1)S(1)}, u32[]{:S(2)}, u32[]{:S(2)}) collective-permute-start(bf16[256,1280]{1,0:T(8,128)(2,1)S(1)} %collective-permute-done.7.refs_3_), channel_id=1, source_target_pairs={{0,8},{8,0},{1,9},{9,1},{2,10},{10,2},{3,11},{11,3},{4,12},{12,4},... | collective-permute-start | bytes 1966088 | tf_op jit(solution)/shard_map/ppermute | solution.py:29
  61.7 18.5 %collective-permute-start.13 = (bf16[640,640]{1,0:T(8,128)(2,1)S(1)}, bf16[640,640]{1,0:T(8,128)(2,1)S(1)}, u32[]{:S(2)}, u32[]{:S(2)}) collective-permute-start(bf16[640,640]{1,0:T(8,128)(2,1)S(1)} %collective-permute-done.3.refs_1_), channel_id=1, source_target_pairs={{0,8},{8,0},{1,9},{9,1},{2,10},{10,2},{3,11},{11,3},{4,12},{12,4},... | collective-permute-start | bytes 2457608 | tf_op jit(solution)/shard_map/ppermute | solution.py:29
  61.7 18.5 %collective-permute-start.14 = (bf16[640,640]{1,0:T(8,128)(2,1)S(1)}, bf16[640,640]{1,0:T(8,128)(2,1)S(1)}, u32[]{:S(2)}, u32[]{:S(2)}) collective-permute-start(bf16[640,640]{1,0:T(8,128)(2,1)S(1)} %collective-permute-done.4.refs_3_), channel_id=1, source_target_pairs={{0,8},{8,0},{1,9},{9,1},{2,10},{10,2},{3,11},{11,3},{4,12},{12,4},... | collective-permute-start | bytes 2457608 | tf_op jit(solution)/shard_map/ppermute | solution.py:29
  65.0 15.2 %collective-permute-start.15 = (bf16[640,640]{1,0:T(8,128)(2,1)S(1)}, bf16[640,640]{1,0:T(8,128)(2,1)S(1)}, u32[]{:S(2)}, u32[]{:S(2)}) collective-permute-start(bf16[640,640]{1,0:T(8,128)(2,1)S(1)} %collective-permute-done.12.refs_2_), channel_id=1, source_target_pairs={{0,8},{8,0},{1,9},{9,1},{2,10},{10,2},{3,11},{11,3},{4,12},{12,4},... | collective-permute-start | bytes 2457608 | tf_op jit(solution)/shard_map/ppermute | solution.py:29
  66.5 13.8 %collective-permute-start.16 = (bf16[256,768]{1,0:T(8,128)(2,1)S(1)}, bf16[256,768]{1,0:T(8,128)(2,1)S(1)}, u32[]{:S(2)}, u32[]{:S(2)}) collective-permute-start(bf16[256,768]{1,0:T(8,128)(2,1)S(1)} %shard_map.70), channel_id=1, source_target_pairs={{0,16},{16,0},{1,17},{17,1},{2,18},{18,2},{3,19},{19,3},{4,20},{20... | collective-permute-start | bytes 1179656 | tf_op jit(solution)/shard_map/ppermute | solution.py:29
  71.2 16.8 %collective-permute-start.22 = (bf16[256,768]{1,0:T(8,128)(2,1)S(1)}, bf16[256,768]{1,0:T(8,128)(2,1)S(1)}, u32[]{:S(2)}, u32[]{:S(2)}) collective-permute-start(bf16[256,768]{1,0:T(8,128)(2,1)S(1)} %shard_map.71), channel_id=1, source_target_pairs={{0,16},{16,0},{1,17},{17,1},{2,18},{18,2},{3,19},{19,3},{4,20},{20... | collective-permute-start | bytes 1179656 | tf_op jit(solution)/shard_map/ppermute | solution.py:29
  80.9 10.7 %collective-permute-start.17 = (bf16[256,640]{1,0:T(8,128)(2,1)S(1)}, bf16[256,640]{1,0:T(8,128)(2,1)S(1)}, u32[]{:S(2)}, u32[]{:S(2)}) collective-permute-start(bf16[256,640]{1,0:T(8,128)(2,1)S(1)} %shard_map.74.refs_8_), channel_id=1, source_target_pairs={{0,3},{1,0},{2,1},{3,2},{4,7},{5,4},{6,5},{7,6},{8,11},{9,8},{10,9... | collective-permute-start | bytes 983048 | tf_op jit(solution)/shard_map/ppermute | solution.py:29
  83.9 11.0 %collective-permute-start.19 = (bf16[256,640]{1,0:T(8,128)(2,1)S(1)}, bf16[256,640]{1,0:T(8,128)(2,1)S(1)}, u32[]{:S(2)}, u32[]{:S(2)}) collective-permute-start(bf16[256,640]{1,0:T(8,128)(2,1)S(1)} %shard_map.74.refs_8_), channel_id=1, source_target_pairs={{0,1},{1,2},{2,3},{3,0},{4,5},{5,6},{6,7},{7,4},{8,9},{9,10},{10,1... | collective-permute-start | bytes 983048 | tf_op jit(solution)/shard_map/ppermute | solution.py:29
  88.6 19.5 %collective-permute-start.23 = (bf16[256,640]{1,0:T(8,128)(2,1)S(1)}, bf16[256,640]{1,0:T(8,128)(2,1)S(1)}, u32[]{:S(2)}, u32[]{:S(2)}) collective-permute-start(bf16[256,640]{1,0:T(8,128)(2,1)S(1)} %shard_map.77.refs_8_), channel_id=1, source_target_pairs={{0,3},{1,0},{2,1},{3,2},{4,7},{5,4},{6,5},{7,6},{8,11},{9,8},{10,9... | collective-permute-start | bytes 983048 | tf_op jit(solution)/shard_map/ppermute | solution.py:29
  91.6 16.8 %collective-permute-start.25 = (bf16[256,640]{1,0:T(8,128)(2,1)S(1)}, bf16[256,640]{1,0:T(8,128)(2,1)S(1)}, u32[]{:S(2)}, u32[]{:S(2)}) collective-permute-start(bf16[256,640]{1,0:T(8,128)(2,1)S(1)} %shard_map.77.refs_8_), channel_id=1, source_target_pairs={{0,1},{1,2},{2,3},{3,0},{4,5},{5,6},{6,7},{7,4},{8,9},{9,10},{10,1... | collective-permute-start | bytes 983048 | tf_op jit(solution)/shard_map/ppermute | solution.py:29
  91.6 10.3 %collective-permute-start.18 = (bf16[128,640]{1,0:T(8,128)(2,1)S(1)}, bf16[128,640]{1,0:T(8,128)(2,1)S(1)}, u32[]{:S(2)}, u32[]{:S(2)}) collective-permute-start(bf16[128,640]{1,0:T(8,128)(2,1)S(1)} %slice.24), channel_id=1, source_target_pairs={{0,3},{1,0},{2,1},{3,2},{4,7},{5,4},{6,5},{7,6},{8,11},{9,8},{10,9... | collective-permute-start | bytes 491528 | tf_op jit(solution)/shard_map/ppermute | solution.py:29
  95.0 10.4 %collective-permute-start.20 = (bf16[128,640]{1,0:T(8,128)(2,1)S(1)}, bf16[128,640]{1,0:T(8,128)(2,1)S(1)}, u32[]{:S(2)}, u32[]{:S(2)}) collective-permute-start(bf16[128,640]{1,0:T(8,128)(2,1)S(1)} %slice.25), channel_id=1, source_target_pairs={{0,1},{1,2},{2,3},{3,0},{4,5},{5,6},{6,7},{7,4},{8,9},{9,10},{10,1... | collective-permute-start | bytes 491528 | tf_op jit(solution)/shard_map/ppermute | solution.py:29
  106.7 13.2 %collective-permute-start.21 = (bf16[256,640]{1,0:T(8,128)(2,1)S(1)}, bf16[256,640]{1,0:T(8,128)(2,1)S(1)}, u32[]{:S(2)}, u32[]{:S(2)}) collective-permute-start(bf16[256,640]{1,0:T(8,128)(2,1)S(1)} %shard_map.76), channel_id=1, source_target_pairs={{0,4},{4,0},{1,5},{5,1},{2,6},{6,2},{3,7},{7,3},{8,12},{12,8},{9,1... | collective-permute-start | bytes 983048 | tf_op jit(solution)/shard_map/ppermute | solution.py:29
  108.1 5.4 %collective-permute-start.24 = (bf16[128,640]{1,0:T(8,128)(2,1)S(1)}, bf16[128,640]{1,0:T(8,128)(2,1)S(1)}, u32[]{:S(2)}, u32[]{:S(2)}) collective-permute-start(bf16[128,640]{1,0:T(8,128)(2,1)S(1)} %slice.26), channel_id=1, source_target_pairs={{0,3},{1,0},{2,1},{3,2},{4,7},{5,4},{6,5},{7,6},{8,11},{9,8},{10,9... | collective-permute-start | bytes 491528 | tf_op jit(solution)/shard_map/ppermute | solution.py:29
  108.5 6.6 %collective-permute-start.26 = (bf16[128,640]{1,0:T(8,128)(2,1)S(1)}, bf16[128,640]{1,0:T(8,128)(2,1)S(1)}, u32[]{:S(2)}, u32[]{:S(2)}) collective-permute-start(bf16[128,640]{1,0:T(8,128)(2,1)S(1)} %slice.27), channel_id=1, source_target_pairs={{0,1},{1,2},{2,3},{3,0},{4,5},{5,6},{6,7},{7,4},{8,9},{9,10},{10,1... | collective-permute-start | bytes 491528 | tf_op jit(solution)/shard_map/ppermute | solution.py:29
  116.4 7.2 %collective-permute-start.27 = (bf16[256,640]{1,0:T(8,128)(2,1)S(1)}, bf16[256,640]{1,0:T(8,128)(2,1)S(1)}, u32[]{:S(2)}, u32[]{:S(2)}) collective-permute-start(bf16[256,640]{1,0:T(8,128)(2,1)S(1)} %shard_map.79), channel_id=1, source_target_pairs={{0,4},{4,0},{1,5},{5,1},{2,6},{6,2},{3,7},{7,3},{8,12},{12,8},{9,1... | collective-permute-start | bytes 983048 | tf_op jit(solution)/shard_map/ppermute | solution.py:29
  (1 other events, 1.1 us)

commit v2 on v1

--- a/solution.py
+++ b/solution.py
@@ -87,20 +87,13 @@
 
 
 def attention_kernel(first, count_q, slots, state_at, last, k_mask, q_frame, *refs):
-    q_parts, kv_parts = refs[:2], refs[2 : 2 + len(slots)]
-    rest = refs[2 + len(slots) :]
+    queries, kv_parts = refs[0], refs[1 : 1 + len(slots)]
+    rest = refs[1 + len(slots) :]
     if state_at is not None:
         o_in, log_in = rest[:2]
         rest = rest[2:]
     out = rest[0]
-    part, part_rows = first // 2, (first % 2) * BLOCK
-    if count_q > 2:
-        queries = rest[-1]
-        queries[:512, :] = q_parts[0][...]
-        queries[512:, :] = q_parts[1][...]
-        part_rows = 0
-    else:
-        queries = q_parts[part]
+    part_rows = (first % 2) * BLOCK
     hidden = jnp.concatenate(
         [k_mask[pl.ds(n * BLOCK, ref.shape[0]), :] for n, ref in zip(slots, kv_parts)], axis=0
     )
@@ -183,12 +176,11 @@
             attention_kernel, first, count_q, slots, state_at if state else None, last
         ),
         out_shape=out_shape,
-        in_specs=[VMEM] * (4 + len(kv_parts) + len(state)),
+        in_specs=[VMEM] * (3 + len(kv_parts) + len(state)),
         out_specs=(VMEM,) * len(out_shape),
-        scratch_shapes=[pltpu.VMEM((rows, WIDTH), jnp.bfloat16)] if count_q > 2 else [],
         compiler_params=pltpu.CompilerParams(vmem_limit_bytes=30 * MIB),
         cost_estimate=SMALL,
-    )(*tabled, *q_parts, *(part for _, part in kv_parts), *state)
+    )(*tabled, q_parts[first // 2], *(part for _, part in kv_parts), *state)
 
 
 def merge_kernel(mine, theirs, out):
@@ -246,25 +238,26 @@
         scratch_shapes=[pltpu.SemaphoreType.DMA((2,))],
         compiler_params=pltpu.CompilerParams(vmem_limit_bytes=8 * MIB),
         cost_estimate=SMALL,
-    )(keys, values)
+    )(*(pltpu.with_memory_space_constraint(a, pltpu.HBM) for a in (keys, values)))
 
 
 def project_kernel(give, *refs):
-    mine, other, parts, out_ref = refs[:4], refs[4:8], refs[8:13], refs[13]
+    mine, other, parts, out_ref, far = refs[:4], refs[4:8], refs[8:13], refs[13], refs[14]
+    far[:128, :] = parts[2][...]
+    far[128:, :] = parts[3][...]
     core_at, zl_at = lax.axis_index("core"), lax.axis_index("zl")
 
     def run(weights):
-        rows = [
-            parts[0][...],
-            parts[1][...],
-            jnp.concatenate([parts[2][...], parts[3][...]], axis=0),
-            parts[4][...],
-        ]
-        total = None
-        for row, w in zip(rows, weights):
-            term = jnp.dot(row, w[...], preferred_element_type=jnp.float32)
-            total = term if total is None else total + term
-        out_ref[...] = total.astype(out_ref.dtype)
+        def half(n, carry):
+            rows = pl.ds(pl.multiple_of(n * 128, 128), 128)
+            total = None
+            for part, w in zip((parts[0], parts[1], far, parts[4]), weights):
+                term = jnp.dot(part[rows, :], w[...], preferred_element_type=jnp.float32)
+                total = term if total is None else total + term
+            out_ref[rows, :] = total.astype(out_ref.dtype)
+            return carry
+
+        lax.fori_loop(0, 2, half, 0)
 
     same = core_at == zl_at
 
@@ -283,6 +276,7 @@
         out_shape=jax.ShapeDtypeStruct((BLOCK, 640), dtype),
         in_specs=[VMEM] * 13,
         out_specs=VMEM,
+        scratch_shapes=[pltpu.VMEM((BLOCK, WIDTH), jnp.bfloat16)],
         compiler_params=pltpu.CompilerParams(vmem_limit_bytes=12 * MIB),
         cost_estimate=SMALL,
     )(*w_mine, *w_other, *parts)
@@ -306,21 +300,30 @@
     kv_core = send(kv, "core", 1)
     w_next = send(after(columns(core_at, 3), kv_core), "x", -1)
     w_back = send(after(columns(core_at, 1), kv_core), "x", 1)
-    attend = functools.partial(
-        attention, tabled=tables(order, frame_seq.reshape(64, 128)), q_parts=(q_z, query)
-    )
-    state = attend((0, 4), kv_parts=((0, kv), (2, kv_core)))
-    kv_next, kv_back, w_next, w_back, state = together(kv_next, kv_back, w_next, w_back, state)
+    tabled = tables(order, frame_seq.reshape(64, 128))
+
+    def attend(blocks, **named):
+        return attention(blocks, tabled, (q_z, query), **named)
+
+    near = ((0, kv), (2, kv_core))
+    state = attend((2, 2), kv_parts=near)
+    q_z, state = together(q_z, state)
+    state_z = attend((0, 2), kv_parts=near)
+    kv_next, kv_back, w_next, w_back, state, state_z = together(
+        kv_next, kv_back, w_next, w_back, state, state_z
+    )
 
     far_low = send(kv_next[:BLOCK], "y", -1)
     far_high = send(kv_back[BLOCK:], "y", 1)
     next_core = send(kv_next, "core", 1)
     back_core = send(kv_back, "core", 1)
     w_far = send(after(columns(core_at, 2), w_next), "x", 2)
-    state = attend((0, 4), kv_parts=((4, kv_next), (6, kv_back)), state=state)
+    near = ((4, kv_next), (6, kv_back))
     cores = ((8, next_core), (10, back_core))
-    state_z = attend((0, 2), kv_parts=cores, state=state)
-    far_low, far_high, state_z = together(far_low, far_high, state_z)
+    state_z = attend((0, 2), kv_parts=near + cores, state=state_z)
+    state, state_z = together(state, state_z)
+    state = attend((2, 2), kv_parts=near, state=state, state_at=2)
+    far_low, far_high, state_z, state = together(far_low, far_high, state_z, state)
 
     low_core, high_core = send(far_low, "core", 1), send(far_high, "core", 1)
     w_next_core, w_back_core = send(w_next, "core", 1), send(w_back, "core", 1)
@@ -334,7 +337,7 @@
         (give,) = attend((block, 1), kv_parts=far_core, state=state_z, last=True)
         got.append(send(give, "zh", 1))
         state, give = together(state, give)
-    state = attend((2, 2), kv_parts=cores, state=state)
+    state = attend((2, 2), kv_parts=cores, state=state, state_at=2)
     (keep,) = attend((2, 2), kv_parts=far + far_core, state=state, state_at=2, last=True)
     keep, w_next_core, w_back_core, w_far_core = together(
         keep, w_next_core, w_back_core, w_far_core

time: 125 us -> 122 us (0.976)
  waiting for transfers between devices: 37.9 us -> 34 us
  Pallas kernels: 44.9 us -> 48.6 us
  local copies, waits for them, and re-layouts: 6 us -> 3.82 us
    ppermute x28, waiting for transfers between devices: 37.9 us -> 34 us  [send(): lax.ppermute(value, axis, [(i, (i + step) % size) for i in range(size)])]
    unnamed x10 -> x6, local copies, waits for them, and re-layouts: 2.18 us -> 0.01 us
    pallas_call x8 -> x9, Pallas kernels: 37.3 us -> 38.5 us  [attention(): pl.pallas_call(functools.partial(attention_kernel, first, count_q, slots,...]
  transfers between devices with their start and end apart: 28 -> 28, of which waited for: 9 -> 9; matrix products, arithmetic and copies ran while one was open for 3% -> 3% of each run, Pallas kernels for 36% -> 39%
where the time goes in v2:
time: 122 us
  Pallas kernels  48.6 us (40%)
  starting transfers between devices  34.4 us (28%)
  waiting for transfers between devices  34 us (28%)
  local copies, waits for them, and re-layouts  3.82 us (3%)
    pallas_call x9, Pallas kernels, attention(): pl.pallas_call(functools.partial(attention_kernel, first, count_q, slots,...  38.5 us
    ppermute x28, starting transfers between devices, send(): lax.ppermute(value, axis, [(i, (i + step) % size) for i in range(size)])  34.4 us
    ppermute x28, waiting for transfers between devices, send(): lax.ppermute(value, axis, [(i, (i + step) % size) for i in range(size)])  34 us
    pallas_call x4, Pallas kernels, project(): pl.pallas_call(functools.partial(project_kernel, give), out_shape=jax.Sha...  6.53 us
    dynamic_slice x1, local copies, waits for them, and re-layouts, columns(): lax.dynamic_slice_in_dim(w_out, (zl * 4 + (x_at + distance) % 4) * 640, 6...  2.58 us
  transfers between devices with their start and end apart: 28, of which 9 were waited for; matrix products, arithmetic and copies ran while one was open for 3% of the time, Pallas kernels for 39%

profile of v2, /device:TPU:0, one launch (start us, length us, event | category | flops | bytes accessed | tf_op | source)
XLA Modules:
  0.0 122.1 jit_solution(16408482572143022010)
XLA Ops:
  1.4 3.2 %collective-permute-start = (bf16[512,1280]{1,0:T(8,128)(2,1)S(1)}, bf16[512,1280]{1,0:T(8,128)(2,1)S(1)}, u32[]{:S(2)}, u32[]{:S(2)}) collective-permute-start(bf16[512,1280]{1,0:T(8,128)(2,1)S(1)} %shard_map.64.refs_1_), channel_id=1, source_target_pairs={{0,96},{32,0},{64,32},{96,64},{1,97},{33,1},{65,33},{97,65},{2,98}... | collective-permute-start | bytes 3932168 | tf_op jit(solution)/shard_map/ppermute | solution.py:29
  4.6 2.6 %constant_dynamic-slice_fusion = (bf16[640,640]{1,0:T(8,128)(2,1)S(1)}, bf16[640,640]{1,0:T(8,128)(2,1)S(1)}, bf16[640,640]{1,0:T(8,128)(2,1)S(1)}, bf16[640,640]{1,0:T(8,128)(2,1)S(1)}, bf16[640,640]{1,0:T(8,128)(2,1)S(1)}) fusion(bf16[640,5120]{1,0:T(8,128)(2,1)} %param.11, s32[]{:T(128)S(6)} %select_n.44, s32[]{:T(128)S(6)} %select_n.41, s32[]{:T(128)S(6)} %select_n.39, ...), kind=kLoop, calls=%fused_computation.3 | loop fusion | bytes 8192020 | tf_op jit(solution)/shard_map/dynamic_slice | solution.py:294
  7.2 2.8 %collective-permute-start.3 = (bf16[640,640]{1,0:T(8,128)(2,1)S(1)}, bf16[640,640]{1,0:T(8,128)(2,1)S(1)}, u32[]{:S(2)}, u32[]{:S(2)}) collective-permute-start(bf16[640,640]{1,0:T(8,128)(2,1)S(1)} %get-tuple-element.56), channel_id=1, source_target_pairs={{0,3},{1,0},{2,1},{3,2},{4,7},{5,4},{6,5},{7,6},{8,11},{9,8},{10,9... | collective-permute-start | bytes 2457608 | tf_op jit(solution)/shard_map/ppermute | solution.py:29
  10.0 3.9 %collective-permute-start.5 = (bf16[512,640]{1,0:T(8,128)(2,1)S(1)}, bf16[512,640]{1,0:T(8,128)(2,1)S(1)}, u32[]{:S(2)}, u32[]{:S(2)}) collective-permute-start(bf16[512,640]{1,0:T(8,128)(2,1)S(1)} %copy-done), channel_id=1, source_target_pairs={{0,16},{16,0},{1,17},{17,1},{2,18},{18,2},{3,19},{19,3},{4,20},{20... | collective-permute-start | bytes 1966088 | tf_op jit(solution)/shard_map/ppermute | solution.py:29
  15.0 5.1 %shard_map.66 = (f32[512,640]{1,0:T(8,128)S(1)}, f32[512,128]{1,0:T(8,128)S(1)}) custom-call(bf16[4096,128]{1,0:T(8,128)(2,1)S(1)} %get-tuple-element.58.k_mask, bf16[1024,128]{1,0:T(8,128)(2,1)S(1)} %get-tuple-element.59.q_frame, bf16[512,640]{1,0:T(8,128)(2,1)S(1)} %copy-done, bf16[512,1280]{1,0:T(8,128)(2,1)S(1)} %shard_map.64.refs_1_, ...), custom_call_target="tpu_custom_call" | custom-call | flops 1024 | bytes 1024 | tf_op jit(solution)/shard_map/pallas_call | solution.py:174
  20.1 8.5 %collective-permute-done.5.refs_0_ = bf16[512,640]{1,0:T(8,128)(2,1)S(1)} collective-permute-done((bf16[512,640]{1,0:T(8,128)(2,1)S(1)}, bf16[512,640]{1,0:T(8,128)(2,1)S(1)}, u32[]{:S(2)}, u32[]{:S(2)}) %collective-permute-start.5) | collective-permute-done | bytes 655392 | tf_op jit(solution)/shard_map/ppermute | solution.py:29
  28.7 5.1 %shard_map.67 = (f32[512,640]{1,0:T(8,128)S(1)}, f32[512,128]{1,0:T(8,128)S(1)}) custom-call(bf16[4096,128]{1,0:T(8,128)(2,1)S(1)} %get-tuple-element.58.k_mask, bf16[1024,128]{1,0:T(8,128)(2,1)S(1)} %get-tuple-element.59.q_frame, bf16[512,640]{1,0:T(8,128)(2,1)S(1)} %collective-permute-done.5.refs_0_, bf16[512,1280]{1,0:T(8,128)(2,1)S(1)} %shard_map.64.refs_1_, ...), custom_call_target="tpu_custom_call" | custom-call | flops 1024 | bytes 1024 | tf_op jit(solution)/shard_map/pallas_call | solution.py:174
  33.8 2.9 %collective-permute-done.1.refs_2_ = bf16[512,1280]{1,0:T(8,128)(2,1)} collective-permute-done((bf16[512,1280]{1,0:T(8,128)(2,1)S(1)}, bf16[512,1280]{1,0:T(8,128)(2,1)}, u32[]{:S(2)}, u32[]{:S(2)}) %collective-permute-start.1) | collective-permute-done | bytes 1310752 | tf_op jit(solution)/shard_map/ppermute | solution.py:29
  38.8 1.8 %collective-permute-start.7 = (bf16[256,1280]{1,0:T(8,128)(2,1)S(1)}, bf16[256,1280]{1,0:T(8,128)(2,1)S(1)}, u32[]{:S(2)}, u32[]{:S(2)}) collective-permute-start(bf16[256,1280]{1,0:T(8,128)(2,1)S(1)} %slice.19), channel_id=1, source_target_pairs={{0,32},{32,64},{64,96},{96,0},{1,33},{33,65},{65,97},{97,1},{2,34}... | collective-permute-start | bytes 1966088 | tf_op jit(solution)/shard_map/ppermute | solution.py:29
  40.5 3.0 %collective-permute-start.12 = (bf16[640,640]{1,0:T(8,128)(2,1)S(1)}, bf16[640,640]{1,0:T(8,128)(2,1)S(1)}, u32[]{:S(2)}, u32[]{:S(2)}) collective-permute-start(bf16[640,640]{1,0:T(8,128)(2,1)S(1)} %get-tuple-element.84), channel_id=1, source_target_pairs={{0,2},{1,3},{2,0},{3,1},{4,6},{5,7},{6,4},{7,5},{8,10},{9,11},{10,... | collective-permute-start | bytes 2457608 | tf_op jit(solution)/shard_map/ppermute | solution.py:29
  43.6 8.6 %shard_map.68 = (f32[512,640]{1,0:T(8,128)S(1)}, f32[512,128]{1,0:T(8,128)S(1)}) custom-call(bf16[4096,128]{1,0:T(8,128)(2,1)S(1)} %get-tuple-element.58.k_mask, bf16[1024,128]{1,0:T(8,128)(2,1)S(1)} %get-tuple-element.59.q_frame, bf16[512,640]{1,0:T(8,128)(2,1)S(1)} %collective-permute-done.5.refs_0_, bf16[512,1280]{1,0:T(8,128)(2,1)S(1)} %collective-permute-done.refs_1_, ...), custom_call_target="tpu_custom_call" | custom-call | flops 1024 | bytes 1024 | tf_op jit(solution)/shard_map/pallas_call | solution.py:174
  52.2 5.5 %shard_map.69 = (f32[512,640]{1,0:T(8,128)S(1)}, f32[512,128]{1,0:T(8,128)S(1)}) custom-call(bf16[4096,128]{1,0:T(8,128)(2,1)S(1)} %get-tuple-element.58.k_mask, bf16[1024,128]{1,0:T(8,128)(2,1)S(1)} %get-tuple-element.59.q_frame, bf16[512,640]{1,0:T(8,128)(2,1)S(1)} %copy-done, bf16[512,1280]{1,0:T(8,128)(2,1)S(1)} %collective-permute-done.refs_1_, ...), custom_call_target="tpu_custom_call" | custom-call | flops 1024 | bytes 1024 | tf_op jit(solution)/shard_map/pallas_call | solution.py:174
  58.8 2.7 %shard_map.70 = (f32[512,640]{1,0:T(8,128)S(1)}, f32[512,128]{1,0:T(8,128)S(1)}) custom-call(bf16[4096,128]{1,0:T(8,128)(2,1)S(1)} %get-tuple-element.58.k_mask, bf16[1024,128]{1,0:T(8,128)(2,1)S(1)} %get-tuple-element.59.q_frame, bf16[512,640]{1,0:T(8,128)(2,1)S(1)} %collective-permute-done.5.refs_0_, bf16[256,1280]{1,0:T(8,128)(2,1)S(1)} %collective-permute-done.6.refs_1_, ...), custom_call_target="tpu_custom_call" | custom-call | flops 1024 | bytes 1024 | tf_op jit(solution)/shard_map/pallas_call | solution.py:174
  61.8 1.4 %shard_map.71 = bf16[256,768]{1,0:T(8,128)(2,1)S(1)} custom-call(bf16[4096,128]{1,0:T(8,128)(2,1)S(1)} %get-tuple-element.58.k_mask, bf16[1024,128]{1,0:T(8,128)(2,1)S(1)} %get-tuple-element.59.q_frame, bf16[512,640]{1,0:T(8,128)(2,1)S(1)} %collective-permute-done.5.refs_0_, bf16[256,1280]{1,0:T(8,128)(2,1)S(1)} %collective-permute-done.10.refs_1_.refs_3_, ...), custom_call_target="tpu_custom_call" | custom-call | flops 1024 | bytes 1024 | tf_op jit(solution)/shard_map/pallas_call | solution.py:174
  63.1 4.0 %collective-permute-start.16 = (bf16[256,768]{1,0:T(8,128)(2,1)S(1)}, bf16[256,768]{1,0:T(8,128)(2,1)S(1)}, u32[]{:S(2)}, u32[]{:S(2)}) collective-permute-start(bf16[256,768]{1,0:T(8,128)(2,1)S(1)} %shard_map.71), channel_id=1, source_target_pairs={{0,16},{16,0},{1,17},{17,1},{2,18},{18,2},{3,19},{19,3},{4,20},{20... | collective-permute-start | bytes 1179656 | tf_op jit(solution)/shard_map/ppermute | solution.py:29
  67.1 1.4 %shard_map.72 = bf16[256,768]{1,0:T(8,128)(2,1)S(1)} custom-call(bf16[4096,128]{1,0:T(8,128)(2,1)S(1)} %get-tuple-element.58.k_mask, bf16[1024,128]{1,0:T(8,128)(2,1)S(1)} %get-tuple-element.59.q_frame, bf16[512,640]{1,0:T(8,128)(2,1)S(1)} %collective-permute-done.5.refs_0_, bf16[256,1280]{1,0:T(8,128)(2,1)S(1)} %collective-permute-done.10.refs_1_.refs_3_, ...), custom_call_target="tpu_custom_call" | custom-call | flops 1024 | bytes 1024 | tf_op jit(solution)/shard_map/pallas_call | solution.py:174
  68.8 4.2 %shard_map.73 = (f32[512,640]{1,0:T(8,128)S(1)}, f32[512,128]{1,0:T(8,128)S(1)}) custom-call(bf16[4096,128]{1,0:T(8,128)(2,1)S(1)} %get-tuple-element.58.k_mask, bf16[1024,128]{1,0:T(8,128)(2,1)S(1)} %get-tuple-element.59.q_frame, bf16[512,640]{1,0:T(8,128)(2,1)S(1)} %copy-done, bf16[512,1280]{1,0:T(8,128)(2,1)S(1)} %collective-permute-done.8.refs_3_.refs_1_, ...), custom_call_target="tpu_custom_call" | custom-call | flops 1024 | bytes 1024 | tf_op jit(solution)/shard_map/pallas_call | solution.py:174
  73.0 4.4 %shard_map.74.mine = bf16[512,768]{1,0:T(8,128)(2,1)S(1)} custom-call(bf16[4096,128]{1,0:T(8,128)(2,1)S(1)} %get-tuple-element.58.k_mask, bf16[1024,128]{1,0:T(8,128)(2,1)S(1)} %get-tuple-element.59.q_frame, bf16[512,640]{1,0:T(8,128)(2,1)S(1)} %copy-done, bf16[256,1280]{1,0:T(8,128)(2,1)S(1)} %collective-permute-done.6.refs_1_, ...), custom_call_target="tpu_custom_call" | custom-call | flops 1024 | bytes 1024 | tf_op jit(solution)/shard_map/pallas_call | solution.py:174
  78.1 2.8 %collective-permute-start.17 = (bf16[256,640]{1,0:T(8,128)(2,1)S(1)}, bf16[256,640]{1,0:T(8,128)(2,1)S(1)}, u32[]{:S(2)}, u32[]{:S(2)}) collective-permute-start(bf16[256,640]{1,0:T(8,128)(2,1)S(1)} %shard_map.75.refs_8_), channel_id=1, source_target_pairs={{0,3},{1,0},{2,1},{3,2},{4,7},{5,4},{6,5},{7,6},{8,11},{9,8},{10,9... | collective-permute-start | bytes 983048 | tf_op jit(solution)/shard_map/ppermute | solution.py:29
  80.9 4.4 %collective-permute-done.22.theirs = bf16[256,768]{1,0:T(8,128)(2,1)S(1)} collective-permute-done((bf16[256,768]{1,0:T(8,128)(2,1)S(1)}, bf16[256,768]{1,0:T(8,128)(2,1)S(1)}, u32[]{:S(2)}, u32[]{:S(2)}) %collective-permute-start.22) | collective-permute-done | bytes 393248 | tf_op jit(solution)/shard_map/ppermute | solution.py:29
  85.9 2.8 %collective-permute-start.23 = (bf16[256,640]{1,0:T(8,128)(2,1)S(1)}, bf16[256,640]{1,0:T(8,128)(2,1)S(1)}, u32[]{:S(2)}, u32[]{:S(2)}) collective-permute-start(bf16[256,640]{1,0:T(8,128)(2,1)S(1)} %shard_map.78.refs_8_), channel_id=1, source_target_pairs={{0,3},{1,0},{2,1},{3,2},{4,7},{5,4},{6,5},{7,6},{8,11},{9,8},{10,9... | collective-permute-start | bytes 983048 | tf_op jit(solution)/shard_map/ppermute | solution.py:29
  88.7 3.3 %collective-permute-start.18 = (bf16[128,640]{1,0:T(8,128)(2,1)S(1)}, bf16[128,640]{1,0:T(8,128)(2,1)S(1)}, u32[]{:S(2)}, u32[]{:S(2)}) collective-permute-start(bf16[128,640]{1,0:T(8,128)(2,1)S(1)} %slice.24), channel_id=1, source_target_pairs={{0,3},{1,0},{2,1},{3,2},{4,7},{5,4},{6,5},{7,6},{8,11},{9,8},{10,9... | collective-permute-start | bytes 491528 | tf_op jit(solution)/shard_map/ppermute | solution.py:29
  92.1 7.1 %collective-permute-done.18.refs_10_ = bf16[128,640]{1,0:T(8,128)(2,1)S(1)} collective-permute-done((bf16[128,640]{1,0:T(8,128)(2,1)S(1)}, bf16[128,640]{1,0:T(8,128)(2,1)S(1)}, u32[]{:S(2)}, u32[]{:S(2)}) %collective-permute-start.18) | collective-permute-done | bytes 163872 | tf_op jit(solution)/shard_map/ppermute | solution.py:29
  99.2 3.4 %collective-permute-done.20.refs_11_ = bf16[128,640]{1,0:T(8,128)(2,1)S(1)} collective-permute-done((bf16[128,640]{1,0:T(8,128)(2,1)S(1)}, bf16[128,640]{1,0:T(8,128)(2,1)S(1)}, u32[]{:S(2)}, u32[]{:S(2)}) %collective-permute-start.20) | collective-permute-done | bytes 163872 | tf_op jit(solution)/shard_map/ppermute | solution.py:29
  102.7 1.6 %shard_map.77 = bf16[256,640]{1,0:T(8,128)(2,1)S(1)} custom-call(bf16[640,640]{1,0:T(8,128)(2,1)S(1)} %get-tuple-element.110.refs_0_, bf16[640,640]{1,0:T(8,128)(2,1)S(1)} %collective-permute-done.3.refs_1_, bf16[640,640]{1,0:T(8,128)(2,1)S(1)} %collective-permute-done.12.refs_2_, bf16[640,640]{1,0:T(8,128)(2,1)S(1)} %collective-permute-done.4.refs_3_, ...), custom_call_target="tpu_custom_call" | custom-call | flops 1024 | bytes 1024 | tf_op jit(solution)/shard_map/pallas_call | solution.py:274
  105.8 1.8 %collective-permute-start.26 = (bf16[128,640]{1,0:T(8,128)(2,1)S(1)}, bf16[128,640]{1,0:T(8,128)(2,1)S(1)}, u32[]{:S(2)}, u32[]{:S(2)}) collective-permute-start(bf16[128,640]{1,0:T(8,128)(2,1)S(1)} %slice.27), channel_id=1, source_target_pairs={{0,1},{1,2},{2,3},{3,0},{4,5},{5,6},{6,7},{7,4},{8,9},{9,10},{10,1... | collective-permute-start | bytes 491528 | tf_op jit(solution)/shard_map/ppermute | solution.py:29
  107.6 3.2 %collective-permute-done.24.refs_10_ = bf16[128,640]{1,0:T(8,128)(2,1)S(1)} collective-permute-done((bf16[128,640]{1,0:T(8,128)(2,1)S(1)}, bf16[128,640]{1,0:T(8,128)(2,1)S(1)}, u32[]{:S(2)}, u32[]{:S(2)}) %collective-permute-start.24) | collective-permute-done | bytes 163872 | tf_op jit(solution)/shard_map/ppermute | solution.py:29
  110.8 1.6 %collective-permute-done.26.refs_11_ = bf16[128,640]{1,0:T(8,128)(2,1)S(1)} collective-permute-done((bf16[128,640]{1,0:T(8,128)(2,1)S(1)}, bf16[128,640]{1,0:T(8,128)(2,1)S(1)}, u32[]{:S(2)}, u32[]{:S(2)}) %collective-permute-start.26) | collective-permute-done | bytes 163872 | tf_op jit(solution)/shard_map/ppermute | solution.py:29
  112.4 1.6 %shard_map.80 = bf16[256,640]{1,0:T(8,128)(2,1)S(1)} custom-call(bf16[640,640]{1,0:T(8,128)(2,1)S(1)} %get-tuple-element.110.refs_0_, bf16[640,640]{1,0:T(8,128)(2,1)S(1)} %collective-permute-done.3.refs_1_, bf16[640,640]{1,0:T(8,128)(2,1)S(1)} %collective-permute-done.12.refs_2_, bf16[640,640]{1,0:T(8,128)(2,1)S(1)} %collective-permute-done.4.refs_3_, ...), custom_call_target="tpu_custom_call" | custom-call | flops 1024 | bytes 1024 | tf_op jit(solution)/shard_map/pallas_call | solution.py:274
  115.0 1.8 %shard_map.76 = f32[256,640]{1,0:T(8,128)S(1)} custom-call(bf16[640,640]{1,0:T(8,128)(2,1)S(1)} %get-tuple-element.110.refs_0_, bf16[640,640]{1,0:T(8,128)(2,1)S(1)} %collective-permute-done.3.refs_1_, bf16[640,640]{1,0:T(8,128)(2,1)S(1)} %collective-permute-done.12.refs_2_, bf16[640,640]{1,0:T(8,128)(2,1)S(1)} %collective-permute-done.4.refs_3_, ...), custom_call_target="tpu_custom_call" | custom-call | flops 1024 | bytes 1024 | tf_op jit(solution)/shard_map/pallas_call | solution.py:274
  116.8 1.6 %shard_map.79 = f32[256,640]{1,0:T(8,128)S(1)} custom-call(bf16[640,640]{1,0:T(8,128)(2,1)S(1)} %get-tuple-element.110.refs_0_, bf16[640,640]{1,0:T(8,128)(2,1)S(1)} %collective-permute-done.3.refs_1_, bf16[640,640]{1,0:T(8,128)(2,1)S(1)} %collective-permute-done.12.refs_2_, bf16[640,640]{1,0:T(8,128)(2,1)S(1)} %collective-permute-done.4.refs_3_, ...), custom_call_target="tpu_custom_call" | custom-call | flops 1024 | bytes 1024 | tf_op jit(solution)/shard_map/pallas_call | solution.py:274
  118.5 2.6 %collective-permute-done.27 = bf16[256,640]{1,0:T(8,128)(2,1)S(1)} collective-permute-done((bf16[256,640]{1,0:T(8,128)(2,1)S(1)}, bf16[256,640]{1,0:T(8,128)(2,1)S(1)}, u32[]{:S(2)}, u32[]{:S(2)}) %collective-permute-start.27) | collective-permute-done | bytes 327712 | tf_op jit(solution)/shard_map/ppermute | solution.py:29
  (57 shorter events, 11.0 us)
Async XLA Ops:
  1.3 5.9 %collective-permute-start.2 = (bf16[512,1280]{1,0:T(8,128)(2,1)S(1)}, bf16[512,1280]{1,0:T(8,128)(2,1)}, u32[]{:S(2)}, u32[]{:S(2)}) collective-permute-start(bf16[512,1280]{1,0:T(8,128)(2,1)S(1)} %shard_map.64.refs_1_), channel_id=1, source_target_pairs={{0,8},{8,0},{1,9},{9,1},{2,10},{10,2},{3,11},{11,3},{4,12},{12,4},... | collective-permute-start | bytes 3932168 | tf_op jit(solution)/shard_map/ppermute | solution.py:29
  1.4 32.4 %collective-permute-start = (bf16[512,1280]{1,0:T(8,128)(2,1)S(1)}, bf16[512,1280]{1,0:T(8,128)(2,1)S(1)}, u32[]{:S(2)}, u32[]{:S(2)}) collective-permute-start(bf16[512,1280]{1,0:T(8,128)(2,1)S(1)} %shard_map.64.refs_1_), channel_id=1, source_target_pairs={{0,96},{32,0},{64,32},{96,64},{1,97},{33,1},{65,33},{97,65},{2,98}... | collective-permute-start | bytes 3932168 | tf_op jit(solution)/shard_map/ppermute | solution.py:29
  4.6 32.2 %collective-permute-start.1 = (bf16[512,1280]{1,0:T(8,128)(2,1)S(1)}, bf16[512,1280]{1,0:T(8,128)(2,1)}, u32[]{:S(2)}, u32[]{:S(2)}) collective-permute-start(bf16[512,1280]{1,0:T(8,128)(2,1)S(1)} %shard_map.64.refs_1_), channel_id=1, source_target_pairs={{0,32},{32,64},{64,96},{96,0},{1,33},{33,65},{65,97},{97,1},{2,34}... | collective-permute-start | bytes 3932168 | tf_op jit(solution)/shard_map/ppermute | solution.py:29
  4.6 5.4 %copy-start = (bf16[512,640]{1,0:T(8,128)(2,1)S(1)}, bf16[512,640]{1,0:T(8,128)(2,1)}, u32[]{:S(2)}) copy-start(bf16[512,640]{1,0:T(8,128)(2,1)} %refs_0_.7) | copy-start | bytes 1966084
  4.6 9.3 %copy-start.1 = (s32[8192]{0:T(1024)S(1)}, s32[8192]{0:T(1024)}, u32[]{:S(2)}) copy-start(s32[8192]{0:T(1024)} %param.9) | copy-start | bytes 98308
  4.6 9.3 %copy-start.2 = (s32[32]{0:T(128)S(1)}, s32[32]{0:T(128)}, u32[]{:S(2)}) copy-start(s32[32]{0:T(128)} %order_ref.1) | copy-start | bytes 388
  7.2 29.6 %collective-permute-start.3 = (bf16[640,640]{1,0:T(8,128)(2,1)S(1)}, bf16[640,640]{1,0:T(8,128)(2,1)S(1)}, u32[]{:S(2)}, u32[]{:S(2)}) collective-permute-start(bf16[640,640]{1,0:T(8,128)(2,1)S(1)} %get-tuple-element.56), channel_id=1, source_target_pairs={{0,3},{1,0},{2,1},{3,2},{4,7},{5,4},{6,5},{7,6},{8,11},{9,8},{10,9... | collective-permute-start | bytes 2457608 | tf_op jit(solution)/shard_map/ppermute | solution.py:29
  10.0 26.7 %collective-permute-start.4 = (bf16[640,640]{1,0:T(8,128)(2,1)S(1)}, bf16[640,640]{1,0:T(8,128)(2,1)S(1)}, u32[]{:S(2)}, u32[]{:S(2)}) collective-permute-start(bf16[640,640]{1,0:T(8,128)(2,1)S(1)} %get-tuple-element.57), channel_id=1, source_target_pairs={{0,1},{1,2},{2,3},{3,0},{4,5},{5,6},{6,7},{7,4},{8,9},{9,10},{10,1... | collective-permute-start | bytes 2457608 | tf_op jit(solution)/shard_map/ppermute | solution.py:29
  10.0 18.7 %collective-permute-start.5 = (bf16[512,640]{1,0:T(8,128)(2,1)S(1)}, bf16[512,640]{1,0:T(8,128)(2,1)S(1)}, u32[]{:S(2)}, u32[]{:S(2)}) collective-permute-start(bf16[512,640]{1,0:T(8,128)(2,1)S(1)} %copy-done), channel_id=1, source_target_pairs={{0,16},{16,0},{1,17},{17,1},{2,18},{18,2},{3,19},{19,3},{4,20},{20... | collective-permute-start | bytes 1966088 | tf_op jit(solution)/shard_map/ppermute | solution.py:29
  36.7 6.8 %collective-permute-start.8 = (bf16[512,1280]{1,0:T(8,128)(2,1)S(1)}, bf16[512,1280]{1,0:T(8,128)(2,1)S(1)}, u32[]{:S(2)}, u32[]{:S(2)}) collective-permute-start(bf16[512,1280]{1,0:T(8,128)(2,1)S(1)} %collective-permute-done.refs_1_), channel_id=1, source_target_pairs={{0,8},{8,0},{1,9},{9,1},{2,10},{10,2},{3,11},{11,3},{4,12},{12,4},... | collective-permute-start | bytes 3932168 | tf_op jit(solution)/shard_map/ppermute | solution.py:29
  36.7 6.8 %collective-permute-start.9 = (bf16[512,1280]{1,0:T(8,128)(2,1)}, bf16[512,1280]{1,0:T(8,128)(2,1)S(1)}, u32[]{:S(2)}, u32[]{:S(2)}) collective-permute-start(bf16[512,1280]{1,0:T(8,128)(2,1)} %collective-permute-done.1.refs_2_), channel_id=1, source_target_pairs={{0,8},{8,0},{1,9},{9,1},{2,10},{10,2},{3,11},{11,3},{4,12},{12,4},... | collective-permute-start | bytes 3932168 | tf_op jit(solution)/shard_map/ppermute | solution.py:29
  38.4 19.3 %collective-permute-start.6 = (bf16[256,1280]{1,0:T(8,128)(2,1)S(1)}, bf16[256,1280]{1,0:T(8,128)(2,1)S(1)}, u32[]{:S(2)}, u32[]{:S(2)}) collective-permute-start(bf16[256,1280]{1,0:T(8,128)(2,1)S(1)} %slice.18), channel_id=1, source_target_pairs={{0,96},{32,0},{64,32},{96,64},{1,97},{33,1},{65,33},{97,65},{2,98}... | collective-permute-start | bytes 1966088 | tf_op jit(solution)/shard_map/ppermute | solution.py:29
  38.8 19.0 %collective-permute-start.7 = (bf16[256,1280]{1,0:T(8,128)(2,1)S(1)}, bf16[256,1280]{1,0:T(8,128)(2,1)S(1)}, u32[]{:S(2)}, u32[]{:S(2)}) collective-permute-start(bf16[256,1280]{1,0:T(8,128)(2,1)S(1)} %slice.19), channel_id=1, source_target_pairs={{0,32},{32,64},{64,96},{96,0},{1,33},{33,65},{65,97},{97,1},{2,34}... | collective-permute-start | bytes 1966088 | tf_op jit(solution)/shard_map/ppermute | solution.py:29
  40.5 21.2 %collective-permute-start.12 = (bf16[640,640]{1,0:T(8,128)(2,1)S(1)}, bf16[640,640]{1,0:T(8,128)(2,1)S(1)}, u32[]{:S(2)}, u32[]{:S(2)}) collective-permute-start(bf16[640,640]{1,0:T(8,128)(2,1)S(1)} %get-tuple-element.84), channel_id=1, source_target_pairs={{0,2},{1,3},{2,0},{3,1},{4,6},{5,7},{6,4},{7,5},{8,10},{9,11},{10,... | collective-permute-start | bytes 2457608 | tf_op jit(solution)/shard_map/ppermute | solution.py:29
  57.7 4.0 %collective-permute-start.10 = (bf16[256,1280]{1,0:T(8,128)(2,1)S(1)}, bf16[256,1280]{1,0:T(8,128)(2,1)S(1)}, u32[]{:S(2)}, u32[]{:S(2)}) collective-permute-start(bf16[256,1280]{1,0:T(8,128)(2,1)S(1)} %collective-permute-done.6.refs_1_), channel_id=1, source_target_pairs={{0,8},{8,0},{1,9},{9,1},{2,10},{10,2},{3,11},{11,3},{4,12},{12,4},... | collective-permute-start | bytes 1966088 | tf_op jit(solution)/shard_map/ppermute | solution.py:29
  57.8 3.9 %collective-permute-start.11 = (bf16[256,1280]{1,0:T(8,128)(2,1)S(1)}, bf16[256,1280]{1,0:T(8,128)(2,1)S(1)}, u32[]{:S(2)}, u32[]{:S(2)}) collective-permute-start(bf16[256,1280]{1,0:T(8,128)(2,1)S(1)} %collective-permute-done.7.refs_2_), channel_id=1, source_target_pairs={{0,8},{8,0},{1,9},{9,1},{2,10},{10,2},{3,11},{11,3},{4,12},{12,4},... | collective-permute-start | bytes 1966088 | tf_op jit(solution)/shard_map/ppermute | solution.py:29
  58.3 19.2 %collective-permute-start.13 = (bf16[640,640]{1,0:T(8,128)(2,1)S(1)}, bf16[640,640]{1,0:T(8,128)(2,1)S(1)}, u32[]{:S(2)}, u32[]{:S(2)}) collective-permute-start(bf16[640,640]{1,0:T(8,128)(2,1)S(1)} %collective-permute-done.3.refs_1_), channel_id=1, source_target_pairs={{0,8},{8,0},{1,9},{9,1},{2,10},{10,2},{3,11},{11,3},{4,12},{12,4},... | collective-permute-start | bytes 2457608 | tf_op jit(solution)/shard_map/ppermute | solution.py:29
  58.4 19.1 %collective-permute-start.14 = (bf16[640,640]{1,0:T(8,128)(2,1)S(1)}, bf16[640,640]{1,0:T(8,128)(2,1)S(1)}, u32[]{:S(2)}, u32[]{:S(2)}) collective-permute-start(bf16[640,640]{1,0:T(8,128)(2,1)S(1)} %collective-permute-done.4.refs_3_), channel_id=1, source_target_pairs={{0,8},{8,0},{1,9},{9,1},{2,10},{10,2},{3,11},{11,3},{4,12},{12,4},... | collective-permute-start | bytes 2457608 | tf_op jit(solution)/shard_map/ppermute | solution.py:29
  61.7 15.8 %collective-permute-start.15 = (bf16[640,640]{1,0:T(8,128)(2,1)S(1)}, bf16[640,640]{1,0:T(8,128)(2,1)S(1)}, u32[]{:S(2)}, u32[]{:S(2)}) collective-permute-start(bf16[640,640]{1,0:T(8,128)(2,1)S(1)} %collective-permute-done.12.refs_2_), channel_id=1, source_target_pairs={{0,8},{8,0},{1,9},{9,1},{2,10},{10,2},{3,11},{11,3},{4,12},{12,4},... | collective-permute-start | bytes 2457608 | tf_op jit(solution)/shard_map/ppermute | solution.py:29
  63.1 14.4 %collective-permute-start.16 = (bf16[256,768]{1,0:T(8,128)(2,1)S(1)}, bf16[256,768]{1,0:T(8,128)(2,1)S(1)}, u32[]{:S(2)}, u32[]{:S(2)}) collective-permute-start(bf16[256,768]{1,0:T(8,128)(2,1)S(1)} %shard_map.71), channel_id=1, source_target_pairs={{0,16},{16,0},{1,17},{17,1},{2,18},{18,2},{3,19},{19,3},{4,20},{20... | collective-permute-start | bytes 1179656 | tf_op jit(solution)/shard_map/ppermute | solution.py:29
  68.5 16.8 %collective-permute-start.22 = (bf16[256,768]{1,0:T(8,128)(2,1)S(1)}, bf16[256,768]{1,0:T(8,128)(2,1)S(1)}, u32[]{:S(2)}, u32[]{:S(2)}) collective-permute-start(bf16[256,768]{1,0:T(8,128)(2,1)S(1)} %shard_map.72), channel_id=1, source_target_pairs={{0,16},{16,0},{1,17},{17,1},{2,18},{18,2},{3,19},{19,3},{4,20},{20... | collective-permute-start | bytes 1179656 | tf_op jit(solution)/shard_map/ppermute | solution.py:29
  78.1 10.6 %collective-permute-start.17 = (bf16[256,640]{1,0:T(8,128)(2,1)S(1)}, bf16[256,640]{1,0:T(8,128)(2,1)S(1)}, u32[]{:S(2)}, u32[]{:S(2)}) collective-permute-start(bf16[256,640]{1,0:T(8,128)(2,1)S(1)} %shard_map.75.refs_8_), channel_id=1, source_target_pairs={{0,3},{1,0},{2,1},{3,2},{4,7},{5,4},{6,5},{7,6},{8,11},{9,8},{10,9... | collective-permute-start | bytes 983048 | tf_op jit(solution)/shard_map/ppermute | solution.py:29
  80.9 11.1 %collective-permute-start.19 = (bf16[256,640]{1,0:T(8,128)(2,1)S(1)}, bf16[256,640]{1,0:T(8,128)(2,1)S(1)}, u32[]{:S(2)}, u32[]{:S(2)}) collective-permute-start(bf16[256,640]{1,0:T(8,128)(2,1)S(1)} %shard_map.75.refs_8_), channel_id=1, source_target_pairs={{0,1},{1,2},{2,3},{3,0},{4,5},{5,6},{6,7},{7,4},{8,9},{9,10},{10,1... | collective-permute-start | bytes 983048 | tf_op jit(solution)/shard_map/ppermute | solution.py:29
  85.9 19.5 %collective-permute-start.23 = (bf16[256,640]{1,0:T(8,128)(2,1)S(1)}, bf16[256,640]{1,0:T(8,128)(2,1)S(1)}, u32[]{:S(2)}, u32[]{:S(2)}) collective-permute-start(bf16[256,640]{1,0:T(8,128)(2,1)S(1)} %shard_map.78.refs_8_), channel_id=1, source_target_pairs={{0,3},{1,0},{2,1},{3,2},{4,7},{5,4},{6,5},{7,6},{8,11},{9,8},{10,9... | collective-permute-start | bytes 983048 | tf_op jit(solution)/shard_map/ppermute | solution.py:29
  88.7 17.1 %collective-permute-start.25 = (bf16[256,640]{1,0:T(8,128)(2,1)S(1)}, bf16[256,640]{1,0:T(8,128)(2,1)S(1)}, u32[]{:S(2)}, u32[]{:S(2)}) collective-permute-start(bf16[256,640]{1,0:T(8,128)(2,1)S(1)} %shard_map.78.refs_8_), channel_id=1, source_target_pairs={{0,1},{1,2},{2,3},{3,0},{4,5},{5,6},{6,7},{7,4},{8,9},{9,10},{10,1... | collective-permute-start | bytes 983048 | tf_op jit(solution)/shard_map/ppermute | solution.py:29
  88.7 10.5 %collective-permute-start.18 = (bf16[128,640]{1,0:T(8,128)(2,1)S(1)}, bf16[128,640]{1,0:T(8,128)(2,1)S(1)}, u32[]{:S(2)}, u32[]{:S(2)}) collective-permute-start(bf16[128,640]{1,0:T(8,128)(2,1)S(1)} %slice.24), channel_id=1, source_target_pairs={{0,3},{1,0},{2,1},{3,2},{4,7},{5,4},{6,5},{7,6},{8,11},{9,8},{10,9... | collective-permute-start | bytes 491528 | tf_op jit(solution)/shard_map/ppermute | solution.py:29
  92.1 10.6 %collective-permute-start.20 = (bf16[128,640]{1,0:T(8,128)(2,1)S(1)}, bf16[128,640]{1,0:T(8,128)(2,1)S(1)}, u32[]{:S(2)}, u32[]{:S(2)}) collective-permute-start(bf16[128,640]{1,0:T(8,128)(2,1)S(1)} %slice.25), channel_id=1, source_target_pairs={{0,1},{1,2},{2,3},{3,0},{4,5},{5,6},{6,7},{7,4},{8,9},{9,10},{10,1... | collective-permute-start | bytes 491528 | tf_op jit(solution)/shard_map/ppermute | solution.py:29
  104.2 14.2 %collective-permute-start.21 = (bf16[256,640]{1,0:T(8,128)(2,1)S(1)}, bf16[256,640]{1,0:T(8,128)(2,1)S(1)}, u32[]{:S(2)}, u32[]{:S(2)}) collective-permute-start(bf16[256,640]{1,0:T(8,128)(2,1)S(1)} %shard_map.77), channel_id=1, source_target_pairs={{0,4},{4,0},{1,5},{5,1},{2,6},{6,2},{3,7},{7,3},{8,12},{12,8},{9,1... | collective-permute-start | bytes 983048 | tf_op jit(solution)/shard_map/ppermute | solution.py:29
  105.4 5.4 %collective-permute-start.24 = (bf16[128,640]{1,0:T(8,128)(2,1)S(1)}, bf16[128,640]{1,0:T(8,128)(2,1)S(1)}, u32[]{:S(2)}, u32[]{:S(2)}) collective-permute-start(bf16[128,640]{1,0:T(8,128)(2,1)S(1)} %slice.26), channel_id=1, source_target_pairs={{0,3},{1,0},{2,1},{3,2},{4,7},{5,4},{6,5},{7,6},{8,11},{9,8},{10,9... | collective-permute-start | bytes 491528 | tf_op jit(solution)/shard_map/ppermute | solution.py:29
  105.8 6.6 %collective-permute-start.26 = (bf16[128,640]{1,0:T(8,128)(2,1)S(1)}, bf16[128,640]{1,0:T(8,128)(2,1)S(1)}, u32[]{:S(2)}, u32[]{:S(2)}) collective-permute-start(bf16[128,640]{1,0:T(8,128)(2,1)S(1)} %slice.27), channel_id=1, source_target_pairs={{0,1},{1,2},{2,3},{3,0},{4,5},{5,6},{6,7},{7,4},{8,9},{9,10},{10,1... | collective-permute-start | bytes 491528 | tf_op jit(solution)/shard_map/ppermute | solution.py:29
  114.0 7.2 %collective-permute-start.27 = (bf16[256,640]{1,0:T(8,128)(2,1)S(1)}, bf16[256,640]{1,0:T(8,128)(2,1)S(1)}, u32[]{:S(2)}, u32[]{:S(2)}) collective-permute-start(bf16[256,640]{1,0:T(8,128)(2,1)S(1)} %shard_map.80), channel_id=1, source_target_pairs={{0,4},{4,0},{1,5},{5,1},{2,6},{6,2},{3,7},{7,3},{8,12},{12,8},{9,1... | collective-permute-start | bytes 983048 | tf_op jit(solution)/shard_map/ppermute | solution.py:29
